TPU v7x, 128 devices: a whole 4x4x4 slice. The times are simulated.
128 devices in a mesh: rows: 16 (over z, y), cols: 8 (over x, core).
Axes of the slice: x: 4, y: 4, z: 4, core: 2. Of those that a mesh axis runs over, the one named last changes fastest.
Arguments:
- noise: bfloat16 [6144, 4096], P('rows'), may hold values from -19 to 19
- data: bfloat16 [6144, 4096], P('cols'), may hold values from -6 to 6
- times: float32 [6144], P('rows'), may hold values from 0 to 1
- time_embed: float32 [4096], replicated, may hold values from -4 to 4
- norm_gain: float32 [4096], replicated, may hold values from 0.1 to 1.9
- w_in: bfloat16 [4096, 8192], P('rows', 'cols'), may hold values from -0.09375 to 0.09375
- w_out: bfloat16 [8192, 4096], P('cols', 'rows'), may hold values from -0.0625 to 0.0625
Outputs:
- target: bfloat16 [6144, 4096], P('rows', 'cols')
- grad_in: bfloat16 [4096, 8192], P('rows', 'cols')
- grad_out: bfloat16 [8192, 4096], P('cols', 'rows')
All inputs are finite; a program needn't handle non-finite values.
Results may differ from a plain program's by a relative error of at most 0.018.
Values may be sent and summed in bfloat16 or wider, within the bound.
A program may use at most 128 MiB of HBM per device.

v0:
```python
import math

import jax
import jax.numpy as jnp
from jax import lax
from jax.sharding import PartitionSpec as P

ITERS = 3


EPSILON = 0.01


def per_device(noise, data, times, time_embed, norm_gain, w_in, w_out):
    width = noise.shape[1]
    tokens = noise.shape[0] * lax.axis_size("rows")
    col_count = lax.axis_size("cols")
    col_index = lax.axis_index("cols")
    noise_f = noise.astype(jnp.float32)
    data_f = data.astype(jnp.float32)
    noise_sq = jnp.sum(noise_f * noise_f, axis=1)
    data_sq = jnp.sum(data_f * data_f, axis=1)
    cross = lax.dot_general(
        noise, data, (((1,), (1,)), ((), ())), preferred_element_type=jnp.float32
    )
    cost = (noise_sq[:, None] + data_sq[None, :] - 2.0 * cross) / width
    base = -EPSILON * math.log(tokens)
    row_pot = jnp.zeros((noise.shape[0],), jnp.float32)
    col_pot = jnp.zeros((data.shape[0],), jnp.float32)
    for sweep in range(ITERS):
        col_logits = (row_pot[:, None] - cost) / EPSILON
        col_top = lax.pmax(jnp.max(col_logits, axis=0), "rows")
        col_sum = lax.psum(jnp.sum(jnp.exp(col_logits - col_top[None, :]), axis=0), "rows")
        col_pot = base - EPSILON * (col_top + jnp.log(col_sum))
        row_logits = (col_pot[None, :] - cost) / EPSILON
        row_top = lax.pmax(jnp.max(row_logits, axis=1), "cols")
        row_sum = lax.psum(jnp.sum(jnp.exp(row_logits - row_top[:, None]), axis=1), "cols")
        row_pot = base - EPSILON * (row_top + jnp.log(row_sum))
    coupling = (
        float(tokens) * jnp.exp((row_pot[:, None] + col_pot[None, :] - cost) / EPSILON)
    ).astype(jnp.bfloat16)
    partial_target = jnp.dot(coupling, data, preferred_element_type=jnp.float32)
    share_width = width // col_count
    target = lax.psum(partial_target.astype(jnp.bfloat16), "cols")
    target_out = lax.dynamic_slice_in_dim(target, col_index * share_width, share_width, 1)
    target_v = target.astype(jnp.float32)
    flow = target_v - noise_f
    state = (
        (1.0 - times[:, None]) * noise_f
        + times[:, None] * target_v
        + times[:, None] * time_embed[None, :]
    )
    normed = (
        state
        * lax.rsqrt(jnp.mean(state * state, axis=1, keepdims=True) + 1e-06)
        * norm_gain[None, :]
    ).astype(jnp.bfloat16)
    hidden = jnp.dot(
        normed, lax.all_gather(w_in, "rows", axis=0, tiled=True), preferred_element_type=jnp.float32
    )
    active = jax.nn.gelu(hidden, approximate=True).astype(jnp.bfloat16)
    w_out_whole = lax.all_gather(w_out, "rows", axis=1, tiled=True)
    partial_velocity = jnp.dot(active, w_out_whole, preferred_element_type=jnp.float32)
    root = math.sqrt(tokens)
    velocity = state + lax.psum(partial_velocity.astype(jnp.bfloat16), "cols").astype(jnp.float32)
    slope = ((velocity - flow) / root).astype(jnp.bfloat16)
    back = lax.dot_general(
        slope, w_out_whole, (((1,), (1,)), ((), ())), preferred_element_type=jnp.float32
    )
    _, pullback = jax.vjp(lambda value: jax.nn.gelu(value, approximate=True), hidden)
    slope_hidden = pullback(back)[0].astype(jnp.bfloat16)
    out_terms = lax.dot_general(
        active, slope, (((0,), (0,)), ((), ())), preferred_element_type=jnp.float32
    )
    grad_out = lax.psum_scatter(
        out_terms.astype(jnp.bfloat16), "rows", scatter_dimension=1, tiled=True
    )
    grad_in = lax.psum_scatter(
        lax.dot_general(
            normed, slope_hidden, (((0,), (0,)), ((), ())), preferred_element_type=jnp.float32
        ).astype(jnp.bfloat16),
        "rows",
        scatter_dimension=0,
        tiled=True,
    )
    return (target_out, grad_in, grad_out)


def solution(mesh):
    in_specs = (
        P("rows", None),
        P("cols", None),
        P("rows"),
        P(),
        P(),
        P("rows", "cols"),
        P("cols", "rows"),
    )
    out_specs = (P("rows", "cols"), P("rows", "cols"), P("cols", "rows"))
    return jax.shard_map(
        per_device, mesh=mesh, in_specs=in_specs, out_specs=out_specs, check_vma=False
    )
```

profile of v0, /device:TPU:0, one launch (start us, length us, event | category | flops | bytes accessed | tf_op | source)
XLA Modules:
  0.0 750.9 jit_solution(13449374923609595529)
XLA Ops:
  8.0 0.0 all-reduce.3.cloned.1.call-start
  8.0 0.0 copy-start
  8.1 0.0 copy-start.3
  8.1 4.2 multiply_reduce_fusion
  12.3 0.0 copy-done
  12.3 0.7 fusion.2
  13.0 0.6 copy-done.3
  13.6 2.7 fusion.15
  16.3 42.0 %pmax.42 = f32[768]{0:T(1024)S(1)} all-reduce(f32[768]{0:T(1024)S(1)} %get-tuple-element.3), channel_id=1, replica_groups=mesh['rows'=16,'cols'=8] {'rows'}, use_global_device_ids=true, to_apply=%region_3.0 | all-reduce | flops 768 | bytes 6144 | tf_op jit(solution)/shard_map/pmax | solution.py:32
  58.4 0.3 exponential_reduce_fusion.5
  58.6 35.5 %psum.56 = f32[768]{0:T(1024)S(1)} all-reduce(f32[768]{0:T(1024)S(1)} %exponential_reduce_fusion.5), channel_id=1, replica_groups=mesh['rows'=16,'cols'=8] {'rows'}, use_global_device_ids=true, to_apply=%region_5.0 | all-reduce | flops 768 | bytes 6144 | tf_op jit(solution)/shard_map/psum | solution.py:33
  94.1 0.2 fusion.16
  94.3 12.4 %pmax.43 = f32[384]{0:T(512)S(1)} all-reduce(f32[384]{0:T(512)S(1)} %fusion.16), channel_id=1, replica_groups=mesh['rows'=16,'cols'=8] {'cols'}, use_global_device_ids=true, to_apply=%region_7.0 | all-reduce | flops 384 | bytes 3072 | tf_op jit(solution)/shard_map/pmax | solution.py:36
  106.7 0.4 exponential_reduce_fusion.4
  107.1 12.4 %psum.57 = f32[384]{0:T(512)S(1)} all-reduce(f32[384]{0:T(512)S(1)} %exponential_reduce_fusion.4), channel_id=1, replica_groups=mesh['rows'=16,'cols'=8] {'cols'}, use_global_device_ids=true, to_apply=%region_9.0 | all-reduce | flops 384 | bytes 3072 | tf_op jit(solution)/shard_map/psum | solution.py:37
  119.5 0.2 fusion.17
  119.7 37.5 %pmax.44 = f32[768]{0:T(1024)S(1)} all-reduce(f32[768]{0:T(1024)S(1)} %fusion.17), channel_id=1, replica_groups=mesh['rows'=16,'cols'=8] {'rows'}, use_global_device_ids=true, to_apply=%region_11.0 | all-reduce | flops 768 | bytes 6144 | tf_op jit(solution)/shard_map/pmax | solution.py:32
  157.2 0.3 exponential_reduce_fusion.3
  157.5 35.5 %psum.58 = f32[768]{0:T(1024)S(1)} all-reduce(f32[768]{0:T(1024)S(1)} %exponential_reduce_fusion.3), channel_id=1, replica_groups=mesh['rows'=16,'cols'=8] {'rows'}, use_global_device_ids=true, to_apply=%region_13.0 | all-reduce | flops 768 | bytes 6144 | tf_op jit(solution)/shard_map/psum | solution.py:33
  193.0 0.2 fusion.18
  193.2 12.4 %pmax.45 = f32[384]{0:T(512)S(1)} all-reduce(f32[384]{0:T(512)S(1)} %fusion.18), channel_id=1, replica_groups=mesh['rows'=16,'cols'=8] {'cols'}, use_global_device_ids=true, to_apply=%region_15.0 | all-reduce | flops 384 | bytes 3072 | tf_op jit(solution)/shard_map/pmax | solution.py:36
  205.6 0.4 exponential_reduce_fusion.2
  206.0 12.4 %psum.59 = f32[384]{0:T(512)S(1)} all-reduce(f32[384]{0:T(512)S(1)} %exponential_reduce_fusion.2), channel_id=1, replica_groups=mesh['rows'=16,'cols'=8] {'cols'}, use_global_device_ids=true, to_apply=%region_17.0 | all-reduce | flops 384 | bytes 3072 | tf_op jit(solution)/shard_map/psum | solution.py:37
  218.4 0.2 fusion.19
  218.6 37.5 %pmax.46 = f32[768]{0:T(1024)S(1)} all-reduce(f32[768]{0:T(1024)S(1)} %fusion.19), channel_id=1, replica_groups=mesh['rows'=16,'cols'=8] {'rows'}, use_global_device_ids=true, to_apply=%region_19.0 | all-reduce | flops 768 | bytes 6144 | tf_op jit(solution)/shard_map/pmax | solution.py:32
  256.1 0.3 exponential_reduce_fusion.1
  256.4 35.5 %psum.60 = f32[768]{0:T(1024)S(1)} all-reduce(f32[768]{0:T(1024)S(1)} %exponential_reduce_fusion.1), channel_id=1, replica_groups=mesh['rows'=16,'cols'=8] {'rows'}, use_global_device_ids=true, to_apply=%region_21.0 | all-reduce | flops 768 | bytes 6144 | tf_op jit(solution)/shard_map/psum | solution.py:33
  291.9 0.2 fusion.20
  292.1 12.4 %pmax.47 = f32[384]{0:T(512)S(1)} all-reduce(f32[384]{0:T(512)S(1)} %fusion.20), channel_id=1, replica_groups=mesh['rows'=16,'cols'=8] {'cols'}, use_global_device_ids=true, to_apply=%region_23.0 | all-reduce | flops 384 | bytes 3072 | tf_op jit(solution)/shard_map/pmax | solution.py:36
  304.5 0.4 exponential_reduce_fusion
  304.9 12.4 %psum.61 = f32[384]{0:T(512)S(1)} all-reduce(f32[384]{0:T(512)S(1)} %exponential_reduce_fusion), channel_id=1, replica_groups=mesh['rows'=16,'cols'=8] {'cols'}, use_global_device_ids=true, to_apply=%region_25.0 | all-reduce | flops 384 | bytes 3072 | tf_op jit(solution)/shard_map/psum | solution.py:37
  317.3 7.0 convolution_convert_fusion.3
  324.3 0.0 all-reduce.3.cloned.1.call-update
  324.3 0.0 all-gather.3.cloned.1.call-start
  324.4 0.5 all-gather.3.cloned.1.call-update
  324.9 0.0 all-gather.5.cloned.1.call-start
  325.0 0.5 all-gather.5.cloned.1.call-update
  325.5 0.2 all-reduce.5.cloned.1.call-start
  325.7 0.0 copy-done.8
  325.8 0.0 copy-start.9
  325.8 64.5 %all-reduce.3.cloned.1.call-done = bf16[384,4096]{1,0:T(8,128)(2,1)} async-done(((bf16[384,4096]{1,0:T(8,128)(2,1)}), bf16[384,4096]{1,0:T(8,128)(2,1)}) %all-reduce.3.cloned.1.call-update) | async-done | bytes 3145744 | tf_op jit(solution)/shard_map/psum | solution.py:44
  390.2 0.0 copy-done.1
  390.2 0.0 copy-done.7
  390.3 4.0 multiply_reduce_fusion.1
  394.3 0.0 copy-done.9
  394.3 0.0 copy-done.2
  394.3 3.7 multiply_convert_fusion
  398.0 8.9 %fusion.40 = f32[384,1024]{1,0:T(8,128)} fusion(bf16[384,4096]{1,0:T(8,128)(2,1)} %multiply_convert_fusion, bf16[4096,1024]{1,0:T(8,128)(2,1)} %all-gather.3.cloned.1.call-done), kind=kOutput, calls=%fused_computation.76 | convolution fusion | flops 3221225472 | bytes 13107200 | tf_op jit(solution)/shard_map/dot_general | solution.py:58
  406.9 65.6 %all-gather.5.cloned.1.call-done = bf16[1024,4096]{1,0:T(8,128)(2,1)} async-done(((bf16[1024,256]{1,0:T(8,128)(2,1)}), bf16[1024,4096]{1,0:T(8,128)(2,1)}) %all-gather.5.cloned.1.call-update) | async-done | bytes 8388624 | tf_op jit(solution)/shard_map/all_gather | solution.py:62
  472.5 9.2 %convolution_convert_fusion.2 = bf16[384,4096]{1,0:T(8,128)(2,1)} fusion(bf16[1024,4096]{1,0:T(8,128)(2,1)} %all-gather.5.cloned.1.call-done, f32[384,1024]{1,0:T(8,128)} %fusion.40), kind=kOutput, calls=%fused_computation.15 | convolution fusion | flops 3226337280 | bytes 13107200 | tf_op jit(solution)/shard_map/dot_general | solution.py:63
  481.7 0.0 all-reduce.5.cloned.1.call-update
  481.7 0.3 reduce-scatter.3.cloned.1.call-start
  482.0 68.1 %all-reduce.5.cloned.1.call-done = bf16[384,4096]{1,0:T(8,128)(2,1)} async-done(((bf16[384,4096]{1,0:T(8,128)(2,1)}), bf16[384,4096]{1,0:T(8,128)(2,1)}) %all-reduce.5.cloned.1.call-update) | async-done | bytes 3145744 | tf_op jit(solution)/shard_map/psum | solution.py:65
  550.1 4.8 fusion.5
  554.9 7.0 fusion.41
  561.9 7.5 %convolution_convert_fusion.1 = bf16[4096,1024]{1,0:T(8,128)(2,1)} fusion(bf16[384,4096]{1,0:T(8,128)(2,1)S(1)} %copy-done.4, f32[384,1024]{1,0:T(8,128)S(1)} %copy-done.10, f32[384,1024]{1,0:T(8,128)S(1)} %fusion.41), kind=kOutput, calls=%fused_computation.6 | convolution fusion | flops 3233284096 | bytes 14680064 | tf_op jit(solution)/shard_map/dot_general | solution.py:79
  569.5 0.0 reduce-scatter.3.cloned.1.call-update
  569.5 0.0 reduce-scatter.5.cloned.1.call-start
  569.6 1.8 copy-done.6
  571.4 8.4 %convolution_convert_fusion = bf16[1024,4096]{1,0:T(8,128)(2,1)} fusion(bf16[384,4096]{1,0:T(8,128)(2,1)S(1)} %copy-done.6, f32[384,1024]{1,0:T(8,128)} %fusion.40), kind=kOutput, calls=%fused_computation.5 | convolution fusion | flops 3228958720 | bytes 13107200 | tf_op jit(solution)/shard_map/dot_general | solution.py:72
  579.8 0.0 reduce-scatter.5.cloned.1.call-update
  579.8 1.8 constant_dynamic-slice_fusion
  581.6 73.0 %reduce-scatter.3.cloned.1.call-done = bf16[256,1024]{1,0:T(8,128)(2,1)} async-done(((bf16[4096,1024]{1,0:T(8,128)(2,1)}), bf16[256,1024]{1,0:T(8,128)(2,1)}) %reduce-scatter.3.cloned.1.call-update) | async-done | bytes 524304 | tf_op jit(solution)/shard_map/reduce_scatter | solution.py:78
  654.6 88.7 %reduce-scatter.5.cloned.1.call-done = bf16[1024,256]{1,0:T(8,128)(2,1)} async-done(((bf16[1024,4096]{1,0:T(8,128)(2,1)}), bf16[1024,256]{1,0:T(8,128)(2,1)}) %reduce-scatter.5.cloned.1.call-update) | async-done | bytes 524304 | tf_op jit(solution)/shard_map/reduce_scatter | solution.py:75
  (20 shorter events, 0.1 us)
Async XLA Ops:
  8.0 382.2 %all-reduce.3.cloned.1.call-start = ((), (), s32[]{:S(2)}) async-start(), calls=%async_computation.2 | async-start | bytes 6291456 | tf_op jit(solution)/shard_map/psum | solution.py:44
  8.0 4.3 copy-start
  8.1 5.6 copy-start.3
  324.3 1.4 copy-start.8
  324.3 65.9 %copy-start.1 = (bf16[384,4096]{1,0:T(8,128)(2,1)S(1)}, bf16[384,4096]{1,0:T(8,128)(2,1)}, u32[]{:S(2)}) copy-start(bf16[384,4096]{1,0:T(8,128)(2,1)} %param.7) | copy-start | bytes 9437188
  324.3 65.9 %copy-start.7 = (f32[4096]{0:T(1024)S(1)}, f32[4096]{0:T(1024)}, u32[]{:S(2)}) copy-start(f32[4096]{0:T(1024)} %param.10) | copy-start | bytes 49156
  324.3 73.7 %all-gather.3.cloned.1.call-start = ((), (), s32[]{:S(2)}) async-start(), calls=%async_computation.3 | async-start | bytes 8912896 | tf_op jit(solution)/shard_map/all_gather | solution.py:59
  324.9 147.6 %all-gather.5.cloned.1.call-start = ((), (), s32[]{:S(2)}) async-start(), calls=%async_computation.4 | async-start | bytes 8912896 | tf_op jit(solution)/shard_map/all_gather | solution.py:62
  325.5 224.6 %all-reduce.5.cloned.1.call-start = ((), (), s32[]{:S(2)}) async-start(), calls=%async_computation.5 | async-start | bytes 6291456 | tf_op jit(solution)/shard_map/psum | solution.py:65
  325.8 68.5 %copy-start.9 = (f32[4096]{0:T(1024)S(1)}, f32[4096]{0:T(1024)}, u32[]{:S(2)}) copy-start(f32[4096]{0:T(1024)} %param.11) | copy-start | bytes 49156
  390.2 4.0 copy-start.2
  481.7 172.9 %reduce-scatter.3.cloned.1.call-start = ((), (), s32[]{:S(2)}) async-start(), calls=%async_computation.6 | async-start | bytes 8912896 | tf_op jit(solution)/shard_map/reduce_scatter | solution.py:78
  554.8 7.1 copy-start.5
  554.9 7.1 copy-start.4
  554.9 7.1 copy-start.10
  569.5 1.9 copy-start.6
  569.5 173.8 %reduce-scatter.5.cloned.1.call-start = ((), (), s32[]{:S(2)}) async-start(), calls=%async_computation.7 | async-start | bytes 8912896 | tf_op jit(solution)/shard_map/reduce_scatter | solution.py:75
Sparse Core Ops, SparseCore 0:
  324.5 65.7 all-reduce.2
  481.8 68.2 all-reduce.4
Sparse Core Ops, SparseCore 1:
  327.0 66.2 all-gather.2
  395.2 77.3 all-gather.4
  569.6 84.9 reduce-scatter.2
  658.6 84.7 reduce-scatter.4
where the time goes:
time: 751 us
  waiting for transfers between devices  361 us (48%)
  blocking collectives  298 us (40%)
  matrix products  50.8 us (7%)
  other arithmetic  20.5 us (3%)
  between operations  15.9 us (2%)
    pmax x3, blocking collectives, per_device(): col_top = lax.pmax(jnp.max(col_logits, axis=0), 'rows')  117 us
    psum x3, blocking collectives, per_device(): lax.psum(jnp.sum(jnp.exp(col_logits - col_top[None, :]), axis=0), 'rows')  106 us
    reduce_scatter x1, waiting for transfers between devices, per_device(): lax.psum_scatter(out_terms.astype(jnp.bfloat16), 'rows', scatter_dimensio...  88.7 us
    reduce_scatter x1, waiting for transfers between devices, per_device(): lax.psum_scatter(lax.dot_general(normed, slope_hidden, (((0,), (0,)), (()...  73 us
    psum x1, waiting for transfers between devices, per_device(): lax.psum(partial_velocity.astype(jnp.bfloat16), 'cols').astype(jnp.float32)  68.1 us
    all_gather x1, waiting for transfers between devices, per_device(): w_out_whole = lax.all_gather(w_out, 'rows', axis=1, tiled=True)  65.6 us
    psum x1, waiting for transfers between devices, per_device(): target = lax.psum(partial_target.astype(jnp.bfloat16), 'cols')  64.5 us
    psum x3, blocking collectives, per_device(): lax.psum(jnp.sum(jnp.exp(row_logits - row_top[:, None]), axis=1), 'cols')  37.3 us
  transfers between devices with their start and end apart: 6, of which 5 were waited for; matrix products, arithmetic and copies ran while one was open for 4% of the time, Pallas kernels for 0%

commit v1 on v0

--- a/solution.py
+++ b/solution.py
@@ -1,44 +1,149 @@
+import functools
 import math
 
 import jax
 import jax.numpy as jnp
 from jax import lax
+from jax.experimental import pallas as pl
+from jax.experimental.pallas import tpu as pltpu
 from jax.sharding import PartitionSpec as P
 
 ITERS = 3
-
-
 EPSILON = 0.01
+MESH = pl.DeviceIdType.MESH
+
+
+def sinkhorn_kernel(tokens, n_rows, n_cols, noise_ref, data_ref, p_ref, a_ref, csend, crecv, rsend, rrecv,
+                    cs_sem, cr_sem, rs_sem, rr_sem):
+    row = lax.axis_index("rows")
+    col = lax.axis_index("cols")
+    n, width = noise_ref.shape
+    m = data_ref.shape[0]
+
+    barrier = pltpu.get_barrier_semaphore()
+    for d in range(1, n_rows):
+        pl.semaphore_signal(barrier, inc=1, device_id=(lax.rem(row + d, n_rows), col), device_id_type=MESH)
+    for d in range(1, n_cols):
+        pl.semaphore_signal(barrier, inc=1, device_id=(row, lax.rem(col + d, n_cols)), device_id_type=MESH)
+
+    step = 512
+    a_ref[...] = jnp.zeros_like(a_ref)
+
+    def body(k, carry):
+        nsq, dsq = carry
+        at = pl.ds(pl.multiple_of(k * step, step), step)
+        nk = noise_ref[:, at]
+        dk = data_ref[:, at]
+        a_ref[...] += lax.dot_general(nk, dk, (((1,), (1,)), ((), ())), preferred_element_type=jnp.float32)
+        nf = nk.astype(jnp.float32)
+        df = dk.astype(jnp.float32)
+        nf = nf * nf
+        df = df * df
+        for j in range(step // 128):
+            nsq = nsq + nf[:, j * 128 : (j + 1) * 128]
+            dsq = dsq + df[:, j * 128 : (j + 1) * 128]
+        return nsq, dsq
+
+    nsq, dsq = lax.fori_loop(
+        0, width // step, body, (jnp.zeros((n, 128), jnp.float32), jnp.zeros((m, 128), jnp.float32))
+    )
+    noise_sq = jnp.sum(nsq, axis=1, keepdims=True)
+    data_sq = jnp.sum(dsq.T, axis=0, keepdims=True)
+    a_ref[...] = (noise_sq + data_sq - 2.0 * a_ref[...]) * (1.0 / (width * EPSILON))
+    base = -math.log(tokens)
+
+    pl.semaphore_wait(barrier, n_rows + n_cols - 2)
+
+    f = jnp.zeros((n, 1), jnp.float32)
+    copies = []
+    for it in range(ITERS):
+        x = f - a_ref[...]
+        top = jnp.max(x, axis=0, keepdims=True)
+        tot = jnp.sum(jnp.exp(x - top), axis=0, keepdims=True)
+        csend[it, 0:1, :] = top
+        csend[it, 1:2, :] = tot
+        now = []
+        for d in range(1, n_rows):
+            c = pltpu.make_async_remote_copy(
+                src_ref=csend.at[it], dst_ref=crecv.at[it, d - 1],
+                send_sem=cs_sem.at[it, d - 1], recv_sem=cr_sem.at[it, d - 1],
+                device_id=(lax.rem(row + d, n_rows), col), device_id_type=MESH)
+            c.start()
+            now.append(c)
+        for c in now:
+            c.wait_recv()
+        copies += now
+        got = crecv[it]
+        gt = got[:, 0, :]
+        best = jnp.maximum(top, jnp.max(gt, axis=0, keepdims=True))
+        total = tot * jnp.exp(top - best) + jnp.sum(got[:, 1, :] * jnp.exp(gt - best), axis=0, keepdims=True)
+        g = base - (best + jnp.log(total))
+
+        x = g - a_ref[...]
+        top = jnp.max(x, axis=1, keepdims=True)
+        tot = jnp.sum(jnp.exp(x - top), axis=1, keepdims=True)
+        lane = lax.broadcasted_iota(jnp.int32, (n, 128), 1)
+        both = jnp.where(lane < 64, top, tot).T
+        top = both[0:1]
+        tot = both[64:65]
+        rsend[it, 0:1, :] = top
+        rsend[it, 1:2, :] = tot
+        now = []
+        for d in range(1, n_cols):
+            c = pltpu.make_async_remote_copy(
+                src_ref=rsend.at[it], dst_ref=rrecv.at[it, d - 1],
+                send_sem=rs_sem.at[it, d - 1], recv_sem=rr_sem.at[it, d - 1],
+                device_id=(row, lax.rem(col + d, n_cols)), device_id_type=MESH)
+            c.start()
+            now.append(c)
+        for c in now:
+            c.wait_recv()
+        copies += now
+        got = rrecv[it]
+        gt = got[:, 0, :]
+        best = jnp.maximum(top, jnp.max(gt, axis=0, keepdims=True))
+        total = tot * jnp.exp(top - best) + jnp.sum(got[:, 1, :] * jnp.exp(gt - best), axis=0, keepdims=True)
+        f = jnp.broadcast_to(base - (best + jnp.log(total)), (128, n)).T[:, 0:1]
+    p_ref[...] = (float(tokens) * jnp.exp(f + g - a_ref[...])).astype(jnp.bfloat16)
+    for c in copies:
+        c.wait_send()
+
+
+def couple(noise, data, n_rows, n_cols):
+    n, width = noise.shape
+    m = data.shape[0]
+    vm = pl.BlockSpec(memory_space=pltpu.VMEM)
+    return pl.pallas_call(
+        functools.partial(sinkhorn_kernel, n * n_rows, n_rows, n_cols),
+        out_shape=jax.ShapeDtypeStruct((n, m), jnp.bfloat16),
+        in_specs=[vm] * 2,
+        out_specs=vm,
+        scratch_shapes=[
+            pltpu.VMEM((n, m), jnp.float32),
+            pltpu.VMEM((ITERS, 2, m), jnp.float32),
+            pltpu.VMEM((ITERS, n_rows - 1, 2, m), jnp.float32),
+            pltpu.VMEM((ITERS, 2, n), jnp.float32),
+            pltpu.VMEM((ITERS, n_cols - 1, 2, n), jnp.float32),
+            pltpu.SemaphoreType.DMA((ITERS, n_rows - 1)),
+            pltpu.SemaphoreType.DMA((ITERS, n_rows - 1)),
+            pltpu.SemaphoreType.DMA((ITERS, n_cols - 1)),
+            pltpu.SemaphoreType.DMA((ITERS, n_cols - 1)),
+        ],
+        compiler_params=pltpu.CompilerParams(
+            collective_id=0, has_side_effects=True, vmem_limit_bytes=40 * 2**20
+        ),
+        cost_estimate=pl.CostEstimate(flops=2 * n * m * width * 30, bytes_accessed=2 * (n + m) * width, transcendentals=7 * n * m),
+    )(noise, data)
 
 
 def per_device(noise, data, times, time_embed, norm_gain, w_in, w_out):
     width = noise.shape[1]
-    tokens = noise.shape[0] * lax.axis_size("rows")
+    n_rows = lax.axis_size("rows")
+    tokens = noise.shape[0] * n_rows
     col_count = lax.axis_size("cols")
     col_index = lax.axis_index("cols")
     noise_f = noise.astype(jnp.float32)
-    data_f = data.astype(jnp.float32)
-    noise_sq = jnp.sum(noise_f * noise_f, axis=1)
-    data_sq = jnp.sum(data_f * data_f, axis=1)
-    cross = lax.dot_general(
-        noise, data, (((1,), (1,)), ((), ())), preferred_element_type=jnp.float32
-    )
-    cost = (noise_sq[:, None] + data_sq[None, :] - 2.0 * cross) / width
-    base = -EPSILON * math.log(tokens)
-    row_pot = jnp.zeros((noise.shape[0],), jnp.float32)
-    col_pot = jnp.zeros((data.shape[0],), jnp.float32)
-    for sweep in range(ITERS):
-        col_logits = (row_pot[:, None] - cost) / EPSILON
-        col_top = lax.pmax(jnp.max(col_logits, axis=0), "rows")
-        col_sum = lax.psum(jnp.sum(jnp.exp(col_logits - col_top[None, :]), axis=0), "rows")
-        col_pot = base - EPSILON * (col_top + jnp.log(col_sum))
-        row_logits = (col_pot[None, :] - cost) / EPSILON
-        row_top = lax.pmax(jnp.max(row_logits, axis=1), "cols")
-        row_sum = lax.psum(jnp.sum(jnp.exp(row_logits - row_top[:, None]), axis=1), "cols")
-        row_pot = base - EPSILON * (row_top + jnp.log(row_sum))
-    coupling = (
-        float(tokens) * jnp.exp((row_pot[:, None] + col_pot[None, :] - cost) / EPSILON)
-    ).astype(jnp.bfloat16)
+    coupling = couple(noise, data, n_rows, col_count)
     partial_target = jnp.dot(coupling, data, preferred_element_type=jnp.float32)
     share_width = width // col_count
     target = lax.psum(partial_target.astype(jnp.bfloat16), "cols")

time: 751 us -> 484 us (0.64)
  blocking collectives: 298 us -> 0 us
  Pallas kernels: 0 us -> 39.7 us
  other arithmetic: 20.5 us -> 12.6 us
    pmax x6 -> x0, blocking collectives: 154 us -> none  [the longest x3 117 us: per_device(): col_top = lax.pmax(jnp.max(col_logits, axis=0), 'rows')]
    psum x6 -> x0, blocking collectives: 144 us -> none  [the longest x3 106 us: per_device(): lax.psum(jnp.sum(jnp.exp(col_logits - col_top[None, :]), axis=0), 'rows')]
    pallas_call x0 -> x1, Pallas kernels: none -> 39.7 us  [couple(): pl.pallas_call(functools.partial(sinkhorn_kernel, n * n_rows, n_rows, n_c...]
  transfers between devices with their start and end apart: 6 -> 6, of which waited for: 5 -> 5; matrix products, arithmetic and copies ran while one was open for 4% -> 6% of each run, Pallas kernels for 0% -> 0%
where the time goes in v1:
time: 484 us
  waiting for transfers between devices  362 us (75%)
  matrix products  45.2 us (9%)
  Pallas kernels  39.7 us (8%)
  between operations  15.8 us (3%)
  other arithmetic  12.6 us (3%)
  local copies, waits for them, and re-layouts  8.29 us (2%)
    reduce_scatter x1, waiting for transfers between devices, per_device(): lax.psum_scatter(out_terms.astype(jnp.bfloat16), 'rows', scatter_dimensio...  88.7 us
    reduce_scatter x1, waiting for transfers between devices, per_device(): lax.psum_scatter(lax.dot_general(normed, slope_hidden, (((0,), (0,)), (()...  73 us
    psum x1, waiting for transfers between devices, per_device(): lax.psum(partial_velocity.astype(jnp.bfloat16), 'cols').astype(jnp.float32)  68.1 us
    all_gather x1, waiting for transfers between devices, per_device(): w_out_whole = lax.all_gather(w_out, 'rows', axis=1, tiled=True)  65.5 us
    psum x1, waiting for transfers between devices, per_device(): target = lax.psum(partial_target.astype(jnp.bfloat16), 'cols')  65.5 us
    pallas_call x1, Pallas kernels, couple(): pl.pallas_call(functools.partial(sinkhorn_kernel, n * n_rows, n_rows, n_c...  39.7 us
  transfers between devices with their start and end apart: 6, of which 5 were waited for; matrix products, arithmetic and copies ran while one was open for 6% of the time, Pallas kernels for 0%

profile of v1, /device:TPU:0, one launch (start us, length us, event | category | flops | bytes accessed | tf_op | source)
XLA Modules:
  0.0 484.1 jit_solution(14181230831736123648)
XLA Ops:
  8.0 0.0 all-reduce.3.cloned.1.call-start
  8.0 0.0 copy-start
  8.1 1.9 copy-done
  9.9 0.0 copy-start.2
  9.9 2.8 copy-done.2
  12.7 39.7 %shard_map.94 = bf16[384,768]{1,0:T(8,128)(2,1)S(1)} custom-call(bf16[384,4096]{1,0:T(8,128)(2,1)S(1)} %copy-done, bf16[768,4096]{1,0:T(8,128)(2,1)S(1)} %copy-done.2), custom_call_target="tpu_custom_call" | custom-call | flops 72477573120 | bytes 9437184 | tf_op jit(solution)/shard_map/pallas_call | solution.py:116
  52.4 4.1 convolution_convert_fusion.3
  56.5 0.0 copy-start.8
  56.5 0.0 copy-start.1
  56.5 0.0 copy-start.7
  56.5 0.0 all-reduce.3.cloned.1.call-update
  56.5 0.0 all-gather.3.cloned.1.call-start
  56.6 0.5 all-gather.3.cloned.1.call-update
  57.1 0.0 all-gather.5.cloned.1.call-start
  57.2 0.5 all-gather.5.cloned.1.call-update
  57.7 0.2 all-reduce.5.cloned.1.call-start
  57.9 0.0 copy-done.8
  58.0 0.0 copy-start.9
  58.0 65.5 %all-reduce.3.cloned.1.call-done = bf16[384,4096]{1,0:T(8,128)(2,1)} async-done(((bf16[384,4096]{1,0:T(8,128)(2,1)}), bf16[384,4096]{1,0:T(8,128)(2,1)}) %all-reduce.3.cloned.1.call-update) | async-done | bytes 3145744 | tf_op jit(solution)/shard_map/psum | solution.py:149
  123.4 0.0 copy-done.1
  123.4 0.0 copy-done.7
  123.4 0.0 copy-start.3
  123.4 4.0 multiply_reduce_fusion
  127.5 0.0 copy-done.9
  127.5 0.0 copy-done.3
  127.5 3.8 multiply_convert_fusion
  131.2 0.0 all-gather.3.cloned.1.call-done
  131.2 8.9 %fusion.25 = f32[384,1024]{1,0:T(8,128)} fusion(bf16[384,4096]{1,0:T(8,128)(2,1)} %multiply_convert_fusion, bf16[4096,1024]{1,0:T(8,128)(2,1)} %all-gather.3.cloned.1.call-done), kind=kOutput, calls=%fused_computation.39 | convolution fusion | flops 3221225472 | bytes 13107200 | tf_op jit(solution)/shard_map/dot_general | solution.py:163
  140.1 65.5 %all-gather.5.cloned.1.call-done = bf16[1024,4096]{1,0:T(8,128)(2,1)} async-done(((bf16[1024,256]{1,0:T(8,128)(2,1)}), bf16[1024,4096]{1,0:T(8,128)(2,1)}) %all-gather.5.cloned.1.call-update) | async-done | bytes 8388624 | tf_op jit(solution)/shard_map/all_gather | solution.py:167
  205.7 9.2 %convolution_convert_fusion.2 = bf16[384,4096]{1,0:T(8,128)(2,1)} fusion(bf16[1024,4096]{1,0:T(8,128)(2,1)} %all-gather.5.cloned.1.call-done, f32[384,1024]{1,0:T(8,128)} %fusion.25), kind=kOutput, calls=%fused_computation.12 | convolution fusion | flops 3226337280 | bytes 13107200 | tf_op jit(solution)/shard_map/dot_general | solution.py:168
  214.9 0.0 all-reduce.5.cloned.1.call-update
  214.9 0.3 reduce-scatter.3.cloned.1.call-start
  215.2 68.1 %all-reduce.5.cloned.1.call-done = bf16[384,4096]{1,0:T(8,128)(2,1)} async-done(((bf16[384,4096]{1,0:T(8,128)(2,1)}), bf16[384,4096]{1,0:T(8,128)(2,1)}) %all-reduce.5.cloned.1.call-update) | async-done | bytes 3145744 | tf_op jit(solution)/shard_map/psum | solution.py:170
  283.3 4.8 fusion.4
  288.0 0.0 copy-start.5
  288.1 0.0 copy-start.4
  288.1 0.0 copy-start.10
  288.1 7.0 %fusion.26 = f32[384,1024]{1,0:T(8,128)S(1)} fusion(bf16[384,4096]{1,0:T(8,128)(2,1)S(1)} %fusion.4, bf16[1024,4096]{1,0:T(8,128)(2,1)} %all-gather.5.cloned.1.call-done), kind=kOutput, calls=%fused_computation.40 | convolution fusion | flops 3221225472 | bytes 13107200 | tf_op jit(solution)/shard_map/dot_general | solution.py:172
  295.1 0.0 copy-done.5
  295.1 0.0 copy-done.4
  295.1 0.0 copy-done.10
  295.1 7.5 %convolution_convert_fusion.1 = bf16[4096,1024]{1,0:T(8,128)(2,1)} fusion(bf16[384,4096]{1,0:T(8,128)(2,1)S(1)} %copy-done.4, f32[384,1024]{1,0:T(8,128)S(1)} %copy-done.10, f32[384,1024]{1,0:T(8,128)S(1)} %fusion.26), kind=kOutput, calls=%fused_computation.4 | convolution fusion | flops 3233284096 | bytes 14680064 | tf_op jit(solution)/shard_map/dot_general | solution.py:184
  302.7 0.0 copy-start.6
  302.7 0.0 reduce-scatter.3.cloned.1.call-update
  302.7 0.0 reduce-scatter.5.cloned.1.call-start
  302.7 1.8 copy-done.6
  304.6 8.5 %convolution_convert_fusion = bf16[1024,4096]{1,0:T(8,128)(2,1)} fusion(bf16[384,4096]{1,0:T(8,128)(2,1)S(1)} %copy-done.6, f32[384,1024]{1,0:T(8,128)} %fusion.25), kind=kOutput, calls=%fused_computation.3 | convolution fusion | flops 3228958720 | bytes 13107200 | tf_op jit(solution)/shard_map/dot_general | solution.py:177
  313.1 0.0 reduce-scatter.5.cloned.1.call-update
  313.1 1.8 constant_dynamic-slice_fusion
  314.9 73.0 %reduce-scatter.3.cloned.1.call-done = bf16[256,1024]{1,0:T(8,128)(2,1)} async-done(((bf16[4096,1024]{1,0:T(8,128)(2,1)}), bf16[256,1024]{1,0:T(8,128)(2,1)}) %reduce-scatter.3.cloned.1.call-update) | async-done | bytes 524304 | tf_op jit(solution)/shard_map/reduce_scatter | solution.py:183
  387.8 88.7 %reduce-scatter.5.cloned.1.call-done = bf16[1024,256]{1,0:T(8,128)(2,1)} async-done(((bf16[1024,4096]{1,0:T(8,128)(2,1)}), bf16[1024,256]{1,0:T(8,128)(2,1)}) %reduce-scatter.5.cloned.1.call-update) | async-done | bytes 524304 | tf_op jit(solution)/shard_map/reduce_scatter | solution.py:180
  (2 shorter events, 0.0 us)
Async XLA Ops:
  8.0 115.4 %all-reduce.3.cloned.1.call-start = ((), (), s32[]{:S(2)}) async-start(), calls=%async_computation.2 | async-start | bytes 6291456 | tf_op jit(solution)/shard_map/psum | solution.py:149
  8.0 1.9 copy-start
  9.9 2.8 copy-start.2
  56.5 1.4 copy-start.8
  56.5 66.9 %copy-start.1 = (bf16[384,4096]{1,0:T(8,128)(2,1)S(1)}, bf16[384,4096]{1,0:T(8,128)(2,1)}, u32[]{:S(2)}) copy-start(bf16[384,4096]{1,0:T(8,128)(2,1)} %noise_ref.1) | copy-start | bytes 9437188
  56.5 66.9 %copy-start.7 = (f32[4096]{0:T(1024)S(1)}, f32[4096]{0:T(1024)}, u32[]{:S(2)}) copy-start(f32[4096]{0:T(1024)} %param.10) | copy-start | bytes 49156
  56.5 74.7 %all-gather.3.cloned.1.call-start = ((), (), s32[]{:S(2)}) async-start(), calls=%async_computation.3 | async-start | bytes 8912896 | tf_op jit(solution)/shard_map/all_gather | solution.py:164
  57.1 148.6 %all-gather.5.cloned.1.call-start = ((), (), s32[]{:S(2)}) async-start(), calls=%async_computation.4 | async-start | bytes 8912896 | tf_op jit(solution)/shard_map/all_gather | solution.py:167
  57.7 225.6 %all-reduce.5.cloned.1.call-start = ((), (), s32[]{:S(2)}) async-start(), calls=%async_computation.5 | async-start | bytes 6291456 | tf_op jit(solution)/shard_map/psum | solution.py:170
  58.0 69.5 %copy-start.9 = (f32[4096]{0:T(1024)S(1)}, f32[4096]{0:T(1024)}, u32[]{:S(2)}) copy-start(f32[4096]{0:T(1024)} %param.11) | copy-start | bytes 49156
  123.4 4.0 copy-start.3
  214.9 172.9 %reduce-scatter.3.cloned.1.call-start = ((), (), s32[]{:S(2)}) async-start(), calls=%async_computation.6 | async-start | bytes 8912896 | tf_op jit(solution)/shard_map/reduce_scatter | solution.py:183
  288.0 7.1 %copy-start.5 = (bf16[384,4096]{1,0:T(8,128)(2,1)}, bf16[384,4096]{1,0:T(8,128)(2,1)S(1)}, u32[]{:S(2)}) copy-start(bf16[384,4096]{1,0:T(8,128)(2,1)S(1)} %fusion.4) | copy-start | bytes 9437188
  288.1 7.1 %copy-start.4 = (bf16[384,4096]{1,0:T(8,128)(2,1)S(1)}, bf16[384,4096]{1,0:T(8,128)(2,1)}, u32[]{:S(2)}) copy-start(bf16[384,4096]{1,0:T(8,128)(2,1)} %multiply_convert_fusion) | copy-start | bytes 9437188
  288.1 7.1 %copy-start.10 = (f32[384,1024]{1,0:T(8,128)S(1)}, f32[384,1024]{1,0:T(8,128)}, u32[]{:S(2)}) copy-start(f32[384,1024]{1,0:T(8,128)} %fusion.25) | copy-start | bytes 4718596
  302.7 1.9 copy-start.6
  302.7 173.8 %reduce-scatter.5.cloned.1.call-start = ((), (), s32[]{:S(2)}) async-start(), calls=%async_computation.7 | async-start | bytes 8912896 | tf_op jit(solution)/shard_map/reduce_scatter | solution.py:180
Sparse Core Ops, SparseCore 0:
  56.7 66.7 all-reduce.2
  215.0 68.2 all-reduce.4
Sparse Core Ops, SparseCore 1:
  59.2 67.2 all-gather.2
  128.4 77.3 all-gather.4
  302.8 85.0 reduce-scatter.2
  391.8 84.6 reduce-scatter.4

commit v2 on v0

v2 whole, which is shorter than its diff:
```python
import functools
import math

import jax
import jax.numpy as jnp
from jax import lax
from jax.experimental import pallas as pl
from jax.experimental.pallas import tpu as pltpu
from jax.sharding import PartitionSpec as P

ITERS = 3
EPSILON = 0.01
MESH = pl.DeviceIdType.MESH
F32 = jnp.float32
BF16 = jnp.bfloat16
NT = (((1,), (1,)), ((), ()))
ORDER = (2, 1, 3, 0)


def ring(value):
    return lax.rem(value + 4, 4)


def tall(row, rows):
    return jnp.broadcast_to(row, (128, rows)).T[:, 0:1]


def flat(left, right):
    lane = lax.broadcasted_iota(jnp.int32, (left.shape[0], 128), 1)
    both = jnp.where(lane < 64, left, right).T
    return both[0:1], both[64:65]


def kernel(noise_hbm, data_hbm, times_ref, embed_ref, gain_ref, w_in_hbm, w_out_ref,
           target_ref, gin_ref, gout_ref,
           slopes, dbuf, win, wout, rx, latents, act, hid, back, a_ref, p_ref, state, sh, turned,
           sibs, sibr, xo, xp, xm, rh, rf, own,
           csend, crecv, rsend, rrecv,
           cs, cr, rs, rr, ag_s, ag_r, xs, xr, ug_s, ug_r, gr_s, gr_r, loc, credit):
    n_rows, n_cols = 16, 8
    row = lax.axis_index("rows")
    col = lax.axis_index("cols")
    z, y = row // 4, lax.rem(row, 4)
    xx, core = col // 2, lax.rem(col, 2)
    n, width = noise_hbm.shape
    m = data_hbm.shape[0]
    share = width // n_cols
    wr, ffd = w_in_hbm.shape
    hw = wr // 2
    qw = wr // 4
    hn = n // 2
    tokens = n * n_rows

    def rcopy(src, dst, send, recv, to):
        c = pltpu.make_async_remote_copy(src_ref=src, dst_ref=dst, send_sem=send, recv_sem=recv,
                                         device_id=to, device_id_type=MESH)
        c.start()
        return c

    barrier = pltpu.get_barrier_semaphore()
    for d in range(1, n_rows):
        pl.semaphore_signal(barrier, inc=1, device_id=(lax.rem(row + d, n_rows), col), device_id_type=MESH)
    for d in range(1, n_cols):
        pl.semaphore_signal(barrier, inc=1, device_id=(row, lax.rem(col + d, n_cols)), device_id_type=MESH)

    def mine(i):
        return pl.ds(pl.multiple_of(i * wr, wr), wr)

    w_copy = pltpu.make_async_copy(w_in_hbm, win.at[mine(row)], loc.at[0])
    w_copy.start()

    def noise_copy(q):
        return pltpu.make_async_copy(noise_hbm.at[:, pl.ds(pl.multiple_of(q * share, share), share)],
                                     slopes.at[q], loc.at[1 + q])

    def data_copy(q):
        return pltpu.make_async_copy(data_hbm.at[:, pl.ds(pl.multiple_of(q * 2 * share, 2 * share), 2 * share)],
                                     dbuf.at[pl.ds(pl.multiple_of(q * m, m), m)], loc.at[9 + q])

    for q in range(4):
        noise_copy(2 * q).start()
        noise_copy(2 * q + 1).start()
        data_copy(q).start()
    wout[mine(row)] = w_out_ref[...].astype(F32).T.astype(BF16)
    w_copy.wait()

    def place(path, f, s):
        return s * 4 + f if path == 0 else f * 4 + s

    def here(path):
        return (y, z) if path == 0 else (z, y)

    def piece(ref, path, f, s, part=None):
        off = path * hw + (qw if part == 1 else 0)
        size = hw if part is None else qw
        return ref.at[pl.ds(pl.multiple_of(place(path, ring(f), ring(s)) * wr + off, qw), size)]

    def toward(path, axis, d):
        f, s = here(path)
        if axis == "f":
            return (place(path, ring(f + d), s), col)
        return (place(path, f, ring(s + d)), col)

    gathers = {}

    def gather_round(w, step):
        ref = (win, wout)[w]
        jobs = {
            1: [(0, "f", 1, 0, 0, None), (1, "f", -1, 0, 0, None), (2, "s", 1, 0, 0, None), (3, "s", -1, 0, 0, None)],
            2: [(4, "f", 1, -1, 0, 0), (5, "f", -1, 1, 0, 1),
                (6, "s", 1, -1, 0, None), (7, "s", -1, -1, 0, None), (8, "s", 1, 1, 0, None), (9, "s", -1, 1, 0, None),
                (10, "s", 1, 0, -1, 0), (11, "s", -1, 0, 1, 1)],
            3: [(12, "s", 1, 2, 0, None), (13, "s", -1, 2, 0, None),
                (14, "s", 1, -1, -1, 0), (15, "s", -1, -1, 1, 1), (16, "s", 1, 1, -1, 0), (17, "s", -1, 1, 1, 1)],
            4: [(18, "s", 1, 2, -1, 0), (19, "s", -1, 2, 1, 1)],
        }
        earlier = {1: (), 2: range(0, 4), 3: range(4, 12), 4: range(12, 18), 5: range(18, 20)}[step]
        for path in range(2):
            for i in earlier:
                gathers[w, path, i].wait_recv()
        for job in jobs.get(step, ()):
            for path in range(2):
                i, axis, d, df, ds_, part = job
                f, s = here(path)
                at = piece(ref, path, f + df, s + ds_, part)
                gathers[w, path, i] = rcopy(at, at, ag_s.at[w, path, i], ag_r.at[w, path, i], toward(path, axis, d))

    pl.semaphore_wait(barrier, n_rows + n_cols - 2)
    gather_round(0, 1)

    a_ref[...] = jnp.zeros_like(a_ref)

    def cost_step(q, carry):
        nsq, dsq = carry
        noise_copy(2 * q).wait()
        noise_copy(2 * q + 1).wait()
        data_copy(q).wait()
        for h in range(2):
            nk = slopes[2 * q + h]
            dk = dbuf[pl.ds(pl.multiple_of(q * m, m), m), h * share : (h + 1) * share]
            a_ref[...] += lax.dot_general(nk, dk, NT, preferred_element_type=F32)
            nf = nk.astype(F32)
            df = dk.astype(F32)
            nf = nf * nf
            df = df * df
            for j in range(share // 128):
                nsq = nsq + nf[:, j * 128 : (j + 1) * 128]
                dsq = dsq + df[:, j * 128 : (j + 1) * 128]
        return nsq, dsq

    nsq, dsq = lax.fori_loop(0, 4, cost_step, (jnp.zeros((n, 128), F32), jnp.zeros((m, 128), F32)))
    noise_sq = jnp.sum(nsq, axis=1, keepdims=True)
    data_sq = jnp.sum(dsq.T, axis=0, keepdims=True)
    a_ref[...] = (noise_sq + data_sq - 2.0 * a_ref[...]) * (1.0 / (width * EPSILON))
    base = -math.log(tokens)
    gather_round(0, 2)
    gather_round(1, 1)

    def rows_swap(it):
        for d in range(1, n_rows):
            rcopy(csend.at[it], crecv.at[it, d - 1], cs.at[it], cr.at[it], (lax.rem(row + d, n_rows), col))

    def cols_swap(it):
        for d in range(1, n_cols):
            rcopy(rsend.at[it], rrecv.at[it, d - 1], rs.at[it], rr.at[it], (row, lax.rem(col + d, n_cols)))

    def await_all(ref, sem):
        pltpu.make_async_copy(ref, ref, sem).wait()

    def merge(got, top, tot):
        gt = got[:, 0, :]
        best = jnp.maximum(top, jnp.max(gt, axis=0, keepdims=True))
        total = tot * jnp.exp(top - best) + jnp.sum(got[:, 1, :] * jnp.exp(gt - best), axis=0, keepdims=True)
        return base - (best + jnp.log(total))

    f = jnp.zeros((n, 1), F32)
    g = None
    for it in range(ITERS):
        x = f - a_ref[...]
        top = jnp.max(x, axis=0, keepdims=True)
        tot = jnp.sum(jnp.exp(x - top), axis=0, keepdims=True)
        csend[it, 0:1, :] = top
        csend[it, 1:2, :] = tot
        rows_swap(it)
        if it == 1:
            gather_round(0, 3)
        if it == 2:
            gather_round(0, 4)
        await_all(crecv.at[it], cr.at[it])
        g = merge(crecv[it], top, tot)

        x = g - a_ref[...]
        top = jnp.max(x, axis=1, keepdims=True)
        tot = jnp.sum(jnp.exp(x - top), axis=1, keepdims=True)
        top, tot = flat(top, tot)
        rsend[it, 0:1, :] = top
        rsend[it, 1:2, :] = tot
        cols_swap(it)
        if it == 1:
            gather_round(1, 2)
        await_all(rrecv.at[it], rr.at[it])
        f = tall(merge(rrecv[it], top, tot), n)
    p_ref[...] = (float(tokens) * jnp.exp(f + g - a_ref[...])).astype(BF16)
    for it in range(ITERS):
        await_all(crecv.at[it], cs.at[it])
        await_all(rrecv.at[it], rs.at[it])

    def at_x(d, k):
        return (row, ring(xx + d) * 2 + k)

    def cols_reduce(make, t):
        def copy(i, src, dst, to):
            return rcopy(src, dst, xs.at[t, i], xr.at[t, i], to)

        twin = []
        for i, d in enumerate(ORDER):
            sibs[i] = make(ring(xx + d) * 2 + 1 - core).astype(BF16)
            twin.append(copy(i, sibs.at[i], sibr.at[i], at_x(0, 1 - core)))

        def both(i, d):
            value = make(ring(xx + d) * 2 + core)
            twin[i].wait_recv()
            return value + sibr[i].astype(F32)

        xo[...] = both(0, 2).astype(BF16)
        c4 = copy(4, xo.at[0:hn], rh.at[0], at_x(1, core))
        c5 = copy(5, xo.at[hn:n], rh.at[1], at_x(-1, core))
        xp[...] = both(1, 1).astype(BF16)
        c6 = copy(6, xp.at[hn:n], rf.at[0, hn:n], at_x(1, core))
        xm[...] = both(2, 3).astype(BF16)
        c7 = copy(7, xm.at[0:hn], rf.at[1, 0:hn], at_x(-1, core))
        own[...] = both(3, 0)
        c4.wait_recv()
        xp[0:hn] = (xp[0:hn].astype(F32) + rh[0].astype(F32)).astype(BF16)
        c8 = copy(8, xp.at[0:hn], rf.at[0, 0:hn], at_x(1, core))
        c5.wait_recv()
        xm[hn:n] = (xm[hn:n].astype(F32) + rh[1].astype(F32)).astype(BF16)
        c9 = copy(9, xm.at[hn:n], rf.at[1, hn:n], at_x(-1, core))
        for c in (c6, c7, c8, c9):
            c.wait_recv()
        for c in twin + [c4, c5, c6, c7, c8, c9]:
            c.wait_send()
        return own[...] + rf[0].astype(F32) + rf[1].astype(F32)

    def cols_gather(ref, t, use):
        me = col

        def slot(d, k):
            return ring(xx + d) * 2 + k

        def copy(i, src, to):
            return rcopy(src, src, ug_s.at[t, i], ug_r.at[t, i], to)

        other = 1 - core
        lo, hi = pl.ds(0, hn), pl.ds(hn, hn)
        twin = at_x(0, other)
        c0 = copy(0, ref.at[me], at_x(1, core))
        c1 = copy(1, ref.at[me], at_x(-1, core))
        c2 = copy(2, ref.at[me], twin)
        use(me, True)
        c2.wait_recv()
        use(slot(0, other), False)
        c0.wait_recv()
        c3 = copy(3, ref.at[slot(-1, core), lo], at_x(1, core))
        c5 = copy(5, ref.at[slot(-1, core)], twin)
        c1.wait_recv()
        c4 = copy(4, ref.at[slot(1, core), hi], at_x(-1, core))
        c6 = copy(6, ref.at[slot(1, core)], twin)
        use(slot(-1, core), False)
        use(slot(1, core), False)
        c3.wait_recv()
        c7 = copy(7, ref.at[slot(2, core), lo], twin)
        c4.wait_recv()
        c8 = copy(8, ref.at[slot(2, core), hi], twin)
        c5.wait_recv()
        use(slot(-1, other), False)
        c6.wait_recv()
        use(slot(1, other), False)
        use(slot(2, core), False)
        c7.wait_recv()
        c8.wait_recv()
        use(slot(2, other), False)
        for c in (c0, c1, c2, c3, c4, c5, c6, c7, c8):
            c.wait_send()

    gather_round(1, 3)

    def target_block(fb):
        rows_at = pl.ds(pl.multiple_of(fb // 2 * m, m), m)
        lanes = pl.ds(pl.multiple_of(lax.rem(fb, 2) * share, share), share)
        return jnp.dot(p_ref[...], dbuf[rows_at, lanes], preferred_element_type=F32)

    target_ref[...] = cols_reduce(target_block, 0).astype(BF16)
    target = target_ref[...].astype(F32)
    noise = slopes[col].astype(F32)
    t = tall(times_ref[...], n)
    lanes = pl.ds(pl.multiple_of(col * share, share), share)
    st = (1.0 - t) * noise + t * target + t * embed_ref[:, lanes]
    latents[col] = (st * gain_ref[:, lanes]).astype(BF16)
    state[...] = st - (target - noise)
    part = jnp.sum(st * st, axis=1, keepdims=True)
    part, _ = flat(part, part)
    rsend[ITERS, 0:1, :] = part
    rsend[ITERS, 1:2, :] = part
    cols_swap(ITERS)

    tiles = ffd // 256

    def tile(j):
        return pl.ds(pl.multiple_of(j * 256, 256), 256)

    def block(i):
        return pl.ds(pl.multiple_of(i * share, share), share)

    gather_round(0, 5)

    def use_latent(i, first):
        def step(j, _):
            value = jnp.dot(latents[i], win[block(i), tile(j)], preferred_element_type=F32)
            hid[:, tile(j)] = value if first else hid[:, tile(j)] + value
            return 0

        lax.fori_loop(0, tiles, step, 0)

    cols_gather(latents, 0, use_latent)
    gather_round(1, 4)
    await_all(rrecv.at[ITERS], rr.at[ITERS])
    await_all(rrecv.at[ITERS], rs.at[ITERS])
    square = part + jnp.sum(rrecv[ITERS][:, 0, :], axis=0, keepdims=True)
    scale = tall(lax.rsqrt(square / width + 1e-6), n)

    def gelu_step(j, _):
        h = hid[:, tile(j)] * scale
        c = math.sqrt(2.0 / math.pi)
        h2 = h * h
        th = jnp.tanh(c * (h + 0.044715 * (h2 * h)))
        act[:, tile(j)] = (0.5 * h * (1.0 + th)).astype(BF16)
        slope_of = 0.5 * (1.0 + th) + 0.5 * h * (1.0 - th * th) * (c * (1.0 + (3 * 0.044715) * h2))
        hid[:, tile(j)] = slope_of * scale
        return 0

    lax.fori_loop(0, tiles, gelu_step, 0)
    gather_round(1, 5)

    def velocity_block(fb):
        return lax.dot_general(act[...], wout[block(fb), :], NT, preferred_element_type=F32)

    slopes[col] = ((state[...] + cols_reduce(velocity_block, 1)) * (1.0 / math.sqrt(tokens))).astype(BF16)

    def use_slope(i, _):
        turned[...] = slopes[i].astype(F32).T.astype(BF16)

        def step(j, _):
            dbuf[block(i), tile(j)] = jnp.dot(turned[...], act[:, tile(j)], preferred_element_type=F32).astype(BF16)
            return 0

        lax.fori_loop(0, tiles, step, 0)

    cols_gather(slopes, 1, use_slope)

    def rx_at(ref, path, j, part=None):
        off = qw if part == 1 else 0
        size = hw if part is None else qw
        return ref.at[pl.ds((path * 16 + j) * hw + off, size)]

    scatters = {}

    def scatter(w, step):
        ref = (dbuf, win)[w]
        land = (rx, wout)[w]

        def copy(path, i, src, dst, axis, d):
            scatters[w, path, i] = rcopy(src, dst, gr_s.at[w, path, i], gr_r.at[w, path, i], toward(path, axis, d))

        def got(path, i):
            scatters[w, path, i].wait_recv()

        def add(at, *more):
            value = at[...].astype(F32)
            for r in more:
                value = value + r[...].astype(F32)
            at[...] = value.astype(BF16)

        for path in range(2):
            f, s = here(path)
            if step == 1:
                for j, e in enumerate((2, 1)):
                    copy(path, j, piece(ref, path, f + 2, s + e), rx_at(land, path, j), "f", 1)
                for j, e in enumerate((3, 0)):
                    copy(path, 2 + j, piece(ref, path, f + 2, s + e), rx_at(land, path, 2 + j), "f", -1)
                for e in (3, 0):
                    copy(path, 4 + e, piece(ref, path, f + 1, s + e), rx_at(land, path, 4 + e), "f", 1)
                for e in (2, 1):
                    copy(path, 8 + e, piece(ref, path, f - 1, s + e), rx_at(land, path, 8 + e), "f", -1)
            if step == 2:
                for j in range(2):
                    e = (2, 1)[j]
                    got(path, j)
                    at = piece(ref, path, f + 1, s + e)
                    add(at, rx_at(land, path, j))
                    copy(path, 4 + e, at, rx_at(land, path, 4 + e), "f", 1)
                    e = (3, 0)[j]
                    got(path, 2 + j)
                    at = piece(ref, path, f - 1, s + e)
                    add(at, rx_at(land, path, 2 + j))
                    copy(path, 8 + e, at, rx_at(land, path, 8 + e), "f", -1)
            if step == 3:
                for e in ORDER:
                    got(path, 4 + e)
                    got(path, 8 + e)
                    add(piece(ref, path, f, s + e), rx_at(land, path, 4 + e), rx_at(land, path, 8 + e))
                    if e == 2:
                        copy(path, 12, piece(ref, path, f, s + 2, 0), rx_at(land, path, 12, 0), "s", 1)
                        copy(path, 13, piece(ref, path, f, s + 2, 1), rx_at(land, path, 12, 1), "s", -1)
                    if e == 1:
                        copy(path, 14, piece(ref, path, f, s + 1, 1), rx_at(land, path, 13, 1), "s", 1)
                    if e == 3:
                        copy(path, 15, piece(ref, path, f, s - 1, 0), rx_at(land, path, 14, 0), "s", -1)
            if step == 4:
                got(path, 12)
                at = piece(ref, path, f, s + 1, 0)
                add(at, rx_at(land, path, 12, 0))
                copy(path, 16, at, rx_at(land, path, 13, 0), "s", 1)
                got(path, 13)
                at = piece(ref, path, f, s - 1, 1)
                add(at, rx_at(land, path, 12, 1))
                copy(path, 17, at, rx_at(land, path, 14, 1), "s", -1)
            if step == 5:
                for i in range(14, 18):
                    got(path, i)
                value = (piece(ref, path, f, s)[...].astype(F32) + rx_at(land, path, 13)[...].astype(F32)
                         + rx_at(land, path, 14)[...].astype(F32))
                half = slice(path * hw, (path + 1) * hw)
                if w == 0:
                    gout_ref[:, half] = value.T.astype(BF16)
                else:
                    gin_ref[half, :] = value.astype(BF16)
                for i in range(18):
                    scatters[w, path, i].wait_send()

    scatter(0, 1)

    back[...] = jnp.zeros_like(back)

    def back_step(i, _):
        def step(j, _):
            back[:, tile(j)] += jnp.dot(slopes[i], wout[block(i), tile(j)], preferred_element_type=F32)
            return 0

        return lax.fori_loop(0, tiles, step, 0)

    lax.fori_loop(0, n_cols, back_step, 0)
    for c in gathers.values():
        c.wait_send()
    for path in range(2):
        for d in (1, -1):
            pl.semaphore_signal(credit, inc=1, device_id=toward(path, "f", d), device_id_type=MESH)
    scatter(0, 2)
    sh[...] = (back[...] * hid[...]).astype(BF16)

    def in_step(i, _):
        turned[...] = latents[i].astype(F32).T.astype(BF16)

        def step(j, _):
            win[block(i), tile(j)] = jnp.dot(turned[...], sh[:, tile(j)], preferred_element_type=F32).astype(BF16)
            return 0

        return lax.fori_loop(0, tiles, step, 0)

    lax.fori_loop(0, n_cols, in_step, 0)
    pl.semaphore_wait(credit, 4)
    scatter(1, 1)
    scatter(0, 3)
    scatter(1, 2)
    scatter(0, 4)
    scatter(0, 5)
    scatter(1, 3)
    scatter(1, 4)
    scatter(1, 5)


def per_device(noise, data, times, time_embed, norm_gain, w_in, w_out):
    n, width = noise.shape
    m = data.shape[0]
    wr, ffd = w_in.shape
    share = width // 8
    vm = pl.BlockSpec(memory_space=pltpu.VMEM)
    hbm = pl.BlockSpec(memory_space=pl.ANY)
    dma = pltpu.SemaphoreType.DMA
    return pl.pallas_call(
        kernel,
        out_shape=(
            jax.ShapeDtypeStruct((n, share), BF16),
            jax.ShapeDtypeStruct((wr, ffd), BF16),
            jax.ShapeDtypeStruct((ffd, wr), BF16),
        ),
        in_specs=[hbm, hbm, vm, vm, vm, hbm, vm],
        out_specs=(vm, vm, vm),
        scratch_shapes=[
            pltpu.VMEM((8, n, share), BF16),
            pltpu.VMEM((width, ffd), BF16),
            pltpu.VMEM((width, ffd), BF16),
            pltpu.VMEM((width, ffd), BF16),
            pltpu.VMEM((width, ffd), BF16),
            pltpu.VMEM((8, n, share), BF16),
            pltpu.VMEM((n, ffd), BF16),
            pltpu.VMEM((n, ffd), F32),
            pltpu.VMEM((n, ffd), F32),
            pltpu.VMEM((n, m), F32),
            pltpu.VMEM((n, m), BF16),
            pltpu.VMEM((n, share), F32),
            pltpu.VMEM((n, ffd), BF16),
            pltpu.VMEM((share, n), BF16),
            pltpu.VMEM((4, n, share), BF16),
            pltpu.VMEM((4, n, share), BF16),
            pltpu.VMEM((n, share), BF16),
            pltpu.VMEM((n, share), BF16),
            pltpu.VMEM((n, share), BF16),
            pltpu.VMEM((2, n // 2, share), BF16),
            pltpu.VMEM((2, n, share), BF16),
            pltpu.VMEM((n, share), F32),
            pltpu.VMEM((ITERS, 2, m), F32),
            pltpu.VMEM((ITERS, 15, 2, m), F32),
            pltpu.VMEM((ITERS + 1, 2, n), F32),
            pltpu.VMEM((ITERS + 1, 7, 2, n), F32),
            dma((ITERS,)), dma((ITERS,)), dma((ITERS + 1,)), dma((ITERS + 1,)),
            dma((2, 2, 20)), dma((2, 2, 20)),
            dma((2, 10)), dma((2, 10)),
            dma((2, 9)), dma((2, 9)),
            dma((2, 2, 18)), dma((2, 2, 18)),
            dma((13,)),
            pltpu.SemaphoreType.REGULAR,
        ],
        compiler_params=pltpu.CompilerParams(
            collective_id=0, has_side_effects=True, vmem_limit_bytes=62 * 2**20
        ),
    )(noise, data, times[None, :], time_embed[None, :], norm_gain[None, :], w_in, w_out)


def solution(mesh):
    in_specs = (
        P("rows", None),
        P("cols", None),
        P("rows"),
        P(),
        P(),
        P("rows", "cols"),
        P("cols", "rows"),
    )
    out_specs = (P("rows", "cols"), P("rows", "cols"), P("cols", "rows"))
    return jax.shard_map(
        per_device, mesh=mesh, in_specs=in_specs, out_specs=out_specs, check_vma=False
    )
```

time: 751 us -> 279 us (0.37)
  waiting for transfers between devices: 361 us -> 0 us
  blocking collectives: 298 us -> 0 us
  Pallas kernels: 0 us -> 271 us
  matrix products: 50.8 us -> 0 us
  other arithmetic: 20.5 us -> 0 us
  between operations: 15.9 us -> 0.64 us
    pallas_call x0 -> x1, Pallas kernels: none -> 271 us  [per_device(): pl.pallas_call(kernel, out_shape=(jax.ShapeDtypeStruct((n, share), BF16),...]
    reduce_scatter x2 -> x0, waiting for transfers between devices: 162 us -> none  [the longest x1 88.7 us: per_device(): lax.psum_scatter(out_terms.astype(jnp.bfloat16), 'rows', scatter_dimensio...]
    pmax x6 -> x0, blocking collectives: 154 us -> none  [the longest x3 117 us: per_device(): col_top = lax.pmax(jnp.max(col_logits, axis=0), 'rows')]
    psum x6 -> x0, blocking collectives: 144 us -> none  [the longest x3 106 us: per_device(): lax.psum(jnp.sum(jnp.exp(col_logits - col_top[None, :]), axis=0), 'rows')]
    psum x2 -> x0, waiting for transfers between devices: 133 us -> none  [the longest x1 68.1 us: per_device(): lax.psum(partial_velocity.astype(jnp.bfloat16), 'cols').astype(jnp.float32)]
    all_gather x2 -> x0, waiting for transfers between devices: 65.6 us -> none  [the longest x1 65.6 us: per_device(): w_out_whole = lax.all_gather(w_out, 'rows', axis=1, tiled=True)]
    dot_general x7 -> x0, matrix products: 50.8 us -> none  [the longest x1 9.19 us: per_device(): jnp.dot(active, w_out_whole, preferred_element_type=jnp.float32)]
    reduce_sum x9 -> x0, other arithmetic: 10.9 us -> none  [the longest x1 4.22 us: per_device(): data_sq = jnp.sum(data_f * data_f, axis=1)]
  transfers between devices with their start and end apart: 6 -> 0, of which waited for: 5 -> 0; matrix products, arithmetic and copies ran while one was open for 4% -> 0% of each run, Pallas kernels for 0% -> 0%
where the time goes in v2:
time: 279 us
  Pallas kernels  271 us (97%)
  local copies, waits for them, and re-layouts  6.75 us (2%)
    pallas_call x1, Pallas kernels, per_device(): pl.pallas_call(kernel, out_shape=(jax.ShapeDtypeStruct((n, share), BF16),...  271 us

profile of v2, /device:TPU:0, one launch (start us, length us, event | category | flops | bytes accessed | tf_op | source)
XLA Modules:
  0.0 278.6 jit_solution(10354563247334927034)
XLA Ops:
  0.6 1.2 broadcast_in_dim.9.times_ref
  1.9 271.2 %shard_map.94 = (bf16[384,512]{1,0:T(8,128)(2,1)}, bf16[256,1024]{1,0:T(8,128)(2,1)}, bf16[1024,256]{1,0:T(8,128)(2,1)}) custom-call(bf16[384,4096]{1,0:T(8,128)(2,1)} %noise_hbm.1, bf16[768,4096]{1,0:T(8,128)(2,1)} %data_hbm.1, f32[1,384]{1,0:T(1,128)} %broadcast_in_dim.9.times_ref, f32[1,4096]{1,0:T(1,128)} %bitcast.2, f32[1,4096]{1,0:T(1,128)} %bitcast.3, ...), custom_call_target="tpu_custom_call" | custom-call | tf_op jit(solution)/shard_map/pallas_call | solution.py:490
  273.1 1.8 copy.13
  274.8 1.9 copy.14
  276.7 1.9 copy.15

commit v3 on v2

v3 whole, which is shorter than its diff:
```python
import functools
import math

import jax
import jax.numpy as jnp
from jax import lax
from jax.experimental import pallas as pl
from jax.experimental.pallas import tpu as pltpu
from jax.sharding import PartitionSpec as P

ITERS = 3
EPSILON = 0.01
MESH = pl.DeviceIdType.MESH
F32 = jnp.float32
BF16 = jnp.bfloat16
NT = (((1,), (1,)), ((), ()))
ORDER = (2, 1, 3, 0)


def ring(value):
    return lax.rem(value + 4, 4)


def tall(row, rows):
    return jnp.broadcast_to(row, (128, rows)).T[:, 0:1]


def flat(left, right):
    lane = lax.broadcasted_iota(jnp.int32, (left.shape[0], 128), 1)
    both = jnp.where(lane < 64, left, right).T
    return both[0:1], both[64:65]


def kernel(noise_hbm, data_hbm, times_ref, embed_ref, gain_ref, w_in_hbm, w_out_ref,
           target_ref, gin_ref, gout_ref,
           slopes, dbuf, win, wout, rx, latents, act, hid, back, a_ref, p_ref, state, sh, turned,
           sibs, sibr, xo, xp, xm, rh, rf, own, nsq, dsq, final,
           csend, crecv, rsend, rrecv,
           cs, cr, rs, rr, ag_s, ag_r, xs, xr, ug_s, ug_r, gr_s, gr_r, loc, credit):
    n_rows, n_cols = 16, 8
    row = lax.axis_index("rows")
    col = lax.axis_index("cols")
    z, y = row // 4, lax.rem(row, 4)
    xx, core = col // 2, lax.rem(col, 2)
    n, width = noise_hbm.shape
    m = data_hbm.shape[0]
    share = width // n_cols
    wr, ffd = w_in_hbm.shape
    half = share // 2
    eighth = share // 4
    hn = n // 2
    tokens = n * n_rows

    def rcopy(src, dst, send, recv, to):
        c = pltpu.make_async_remote_copy(src_ref=src, dst_ref=dst, send_sem=send, recv_sem=recv,
                                         device_id=to, device_id_type=MESH)
        c.start()
        return c

    barrier = pltpu.get_barrier_semaphore()
    for d in range(1, n_rows):
        pl.semaphore_signal(barrier, inc=1, device_id=(lax.rem(row + d, n_rows), col), device_id_type=MESH)
    for d in range(1, n_cols):
        pl.semaphore_signal(barrier, inc=1, device_id=(row, lax.rem(col + d, n_cols)), device_id_type=MESH)

    def mine(i):
        return pl.ds(pl.multiple_of(i * wr, wr), wr)

    w_copy = pltpu.make_async_copy(w_in_hbm, win.at[mine(row)], loc.at[0])
    w_copy.start()

    def noise_copy(q):
        return pltpu.make_async_copy(noise_hbm.at[:, pl.ds(pl.multiple_of(q * half, half), half)],
                                     slopes.at[lax.rem(q, 2), q // 2], loc.at[5 + q])

    def data_copy(q):
        return pltpu.make_async_copy(data_hbm.at[:, pl.ds(pl.multiple_of(q * 2 * share, 2 * share), 2 * share)],
                                     dbuf.at[pl.ds(pl.multiple_of(q * m, m), m)], loc.at[1 + q])

    for q in range(4):
        for h in range(4):
            noise_copy(4 * q + h).start()
        data_copy(q).start()
    wout[mine(row)] = w_out_ref[...].astype(F32).T.astype(BF16)
    w_copy.wait()

    def place(path, f, s):
        return s * 4 + f if path == 0 else f * 4 + s

    def here(path):
        return (y, z) if path == 0 else (z, y)

    def piece(ref, unit, path, f, s, part=None):
        base, high = unit
        off = base + path * high + (high // 2 if part == 1 else 0)
        size = high if part is None else high // 2
        return ref.at[pl.ds(pl.multiple_of(place(path, ring(f), ring(s)) * wr + off, high // 2), size)]

    wide, low, up = (0, wr // 2), (0, wr // 4), (wr // 2, wr // 4)

    def toward(path, axis, d):
        f, s = here(path)
        if axis == "f":
            return (place(path, ring(f + d), s), col)
        return (place(path, f, ring(s + d)), col)

    gathers = {}

    def gather(w, *steps):
        ref = (win, wout, wout)[w]
        unit = (wide, low, up)[w]
        jobs = {
            "1": [(0, "f", 1, 0, 0, None), (1, "f", -1, 0, 0, None), (2, "s", 1, 0, 0, None), (3, "s", -1, 0, 0, None)],
            "2a": [(4, "f", 1, -1, 0, 0), (5, "f", -1, 1, 0, 1),
                   (6, "s", 1, -1, 0, None), (7, "s", -1, -1, 0, None), (8, "s", 1, 1, 0, None), (9, "s", -1, 1, 0, None)],
            "2b": [(10, "s", 1, 0, -1, 0), (11, "s", -1, 0, 1, 1)],
            "3a": [(12, "s", 1, 2, 0, None), (13, "s", -1, 2, 0, None)],
            "3b": [(14, "s", 1, -1, -1, 0), (15, "s", -1, -1, 1, 1)],
            "3c": [(16, "s", 1, 1, -1, 0), (17, "s", -1, 1, 1, 1)],
            "4": [(18, "s", 1, 2, -1, 0), (19, "s", -1, 2, 1, 1)],
        }
        needs = {"2a": (0, 1), "2b": (2, 3), "3a": (4, 5), "3b": (6, 7), "3c": (8, 9), "4": (12, 13),
                 "end": (10, 11, 14, 15, 16, 17, 18, 19)}
        for step in steps:
            for i in needs.get(step, ()):
                for path in range(2):
                    gathers[w, path, i].wait_recv()
            for i, axis, d, df, ds_, part in jobs.get(step, ()):
                for path in range(2):
                    f, s = here(path)
                    at = piece(ref, unit, path, f + df, s + ds_, part)
                    gathers[w, path, i] = rcopy(at, at, ag_s.at[w, path, i], ag_r.at[w, path, i], toward(path, axis, d))

    pl.semaphore_wait(barrier, n_rows + n_cols - 2)
    gather(0, "1")
    gather(1, "1")

    def squares(value):
        value = value.astype(F32)
        value = value * value
        out = value[:, 0:128]
        for j in range(1, value.shape[1] // 128):
            out = out + value[:, j * 128 : (j + 1) * 128]
        return out

    for q in range(4):
        for h in range(4):
            noise_copy(4 * q + h).wait()
        data_copy(q).wait()
        total = None
        for h in range(4):
            term = lax.dot_general(slopes[h % 2, 2 * q + h // 2],
                                   dbuf[q * m : (q + 1) * m, h * half : (h + 1) * half], NT,
                                   preferred_element_type=F32)
            total = term if total is None else total + term
        a_ref[...] = total if q == 0 else a_ref[...] + total

        def noise_rows(i, _, q=q):
            at = pl.ds(pl.multiple_of(i * 32, 32), 32)
            value = squares(slopes[0, 2 * q, at, :])
            for h in range(1, 4):
                value = value + squares(slopes[h % 2, 2 * q + h // 2, at, :])
            nsq[at, :] = value if q == 0 else nsq[at, :] + value
            return 0

        def data_rows(i, _, q=q):
            at = pl.ds(pl.multiple_of(i * 32, 32), 32)
            value = squares(dbuf[pl.ds(pl.multiple_of(q * m + i * 32, 32), 32), :])
            dsq[at, :] = value if q == 0 else dsq[at, :] + value
            return 0

        lax.fori_loop(0, n // 32, noise_rows, 0)
        lax.fori_loop(0, m // 32, data_rows, 0)
    noise_sq = jnp.sum(nsq[...], axis=1, keepdims=True)
    data_sq = jnp.sum(dsq[...].T, axis=0, keepdims=True)
    a_ref[...] = (noise_sq + data_sq - 2.0 * a_ref[...]) * (1.0 / (width * EPSILON))
    base = -math.log(tokens)
    gather(0, "2a", "2b")

    def rows_swap(it):
        for d in range(1, n_rows):
            rcopy(csend.at[it], crecv.at[it, d - 1], cs.at[it], cr.at[it], (lax.rem(row + d, n_rows), col))

    def cols_swap(it):
        for d in range(1, n_cols):
            rcopy(rsend.at[it], rrecv.at[it, d - 1], rs.at[it], rr.at[it], (row, lax.rem(col + d, n_cols)))

    def await_all(ref, sem):
        pltpu.make_async_copy(ref, ref, sem).wait()

    def merge(got, top, tot):
        gt = got[:, 0, :]
        best = jnp.maximum(top, jnp.max(gt, axis=0, keepdims=True))
        total = tot * jnp.exp(top - best) + jnp.sum(got[:, 1, :] * jnp.exp(gt - best), axis=0, keepdims=True)
        return base - (best + jnp.log(total))

    f = jnp.zeros((n, 1), F32)
    g = None
    for it in range(ITERS):
        x = f - a_ref[...]
        top = jnp.max(x, axis=0, keepdims=True)
        tot = jnp.sum(jnp.exp(x - top), axis=0, keepdims=True)
        csend[it, 0:1, :] = top
        csend[it, 1:2, :] = tot
        rows_swap(it)
        if it == 2:
            gather(0, "3a", "3b", "3c")
            gather(1, "2a", "2b")
        await_all(crecv.at[it], cr.at[it])
        g = merge(crecv[it], top, tot)

        x = g - a_ref[...]
        top = jnp.max(x, axis=1, keepdims=True)
        tot = jnp.sum(jnp.exp(x - top), axis=1, keepdims=True)
        top, tot = flat(top, tot)
        rsend[it, 0:1, :] = top
        rsend[it, 1:2, :] = tot
        cols_swap(it)
        if it == 0:
            gather(2, "1")
        await_all(rrecv.at[it], rr.at[it])
        f = tall(merge(rrecv[it], top, tot), n)
    p_ref[...] = (float(tokens) * jnp.exp(f + g - a_ref[...])).astype(BF16)
    for it in range(ITERS):
        await_all(crecv.at[it], cs.at[it])
        await_all(rrecv.at[it], rs.at[it])

    def at_x(d, k):
        return (row, ring(xx + d) * 2 + k)

    def cols_reduce(make, t, u):
        def copy(i, src, dst, to):
            return rcopy(src, dst, xs.at[t, u, i], xr.at[t, u, i], to)

        c = {}

        def begin():
            for i, d in enumerate(ORDER):
                sibs[u, i] = make(ring(xx + d) * 2 + 1 - core, u).astype(BF16)
                c[i] = copy(i, sibs.at[u, i], sibr.at[u, i], at_x(0, 1 - core))
                value = make(ring(xx + d) * 2 + core, u)
                c[i].wait_recv()
                value = value + sibr[u, i].astype(F32)
                if d == 0:
                    own[u] = value
                    continue
                out = (xo, xp, None, xm)[i if i < 2 else 3]
                out[u] = value.astype(BF16)
                if d == 2:
                    c[4] = copy(4, out.at[u, 0:hn], rh.at[u, 0], at_x(1, core))
                    c[5] = copy(5, out.at[u, hn:n], rh.at[u, 1], at_x(-1, core))
                elif d == 1:
                    c[6] = copy(6, out.at[u, hn:n], rf.at[u, 0, hn:n], at_x(1, core))
                else:
                    c[7] = copy(7, out.at[u, 0:hn], rf.at[u, 1, 0:hn], at_x(-1, core))

        def middle():
            c[4].wait_recv()
            xp[u, 0:hn] = (xp[u, 0:hn].astype(F32) + rh[u, 0].astype(F32)).astype(BF16)
            c[8] = copy(8, xp.at[u, 0:hn], rf.at[u, 0, 0:hn], at_x(1, core))
            c[5].wait_recv()
            xm[u, hn:n] = (xm[u, hn:n].astype(F32) + rh[u, 1].astype(F32)).astype(BF16)
            c[9] = copy(9, xm.at[u, hn:n], rf.at[u, 1, hn:n], at_x(-1, core))

        def finish():
            for i in (6, 7, 8, 9):
                c[i].wait_recv()
            value = own[u] + rf[u, 0].astype(F32) + rf[u, 1].astype(F32)
            for i in range(10):
                c[i].wait_send()
            return value

        return begin, middle, finish

    def slot(d, k):
        return ring(xx + d) * 2 + k

    other = 1 - core

    def cols_gather(ref, t, u):
        def copy(i, src, to):
            return rcopy(src, src, ug_s.at[t, u, i], ug_r.at[t, u, i], to)

        lo, hi = pl.ds(0, hn), pl.ds(hn, hn)
        twin = at_x(0, other)
        c = {}

        def begin():
            c[0] = copy(0, ref.at[u, col], at_x(1, core))
            c[1] = copy(1, ref.at[u, col], at_x(-1, core))
            c[2] = copy(2, ref.at[u, col], twin)

        def middle():
            c[0].wait_recv()
            c[3] = copy(3, ref.at[u, slot(-1, core), lo], at_x(1, core))
            c[5] = copy(5, ref.at[u, slot(-1, core)], twin)
            c[1].wait_recv()
            c[4] = copy(4, ref.at[u, slot(1, core), hi], at_x(-1, core))
            c[6] = copy(6, ref.at[u, slot(1, core)], twin)

        def finish():
            c[3].wait_recv()
            c[7] = copy(7, ref.at[u, slot(2, core), lo], twin)
            c[4].wait_recv()
            c[8] = copy(8, ref.at[u, slot(2, core), hi], twin)

        def got(*which):
            for i in which:
                c[i].wait_recv()

        def close():
            for i in range(9):
                c[i].wait_send()

        return begin, middle, finish, got, close

    tiles = ffd // 256

    def tile(j):
        return pl.ds(pl.multiple_of(j * 256, 256), 256)

    def rows_of(i, u, size):
        return pl.ds(pl.multiple_of(i * share + u * size, size), size)

    def target_block(fb, u):
        rows_at = pl.ds(pl.multiple_of(fb // 2 * m, m), m)
        lanes = pl.ds(pl.multiple_of(lax.rem(fb, 2) * share + u * half, half), half)
        return jnp.dot(p_ref[...], dbuf[rows_at, lanes], preferred_element_type=F32)

    t = tall(times_ref[...][None, :], n)

    def make_state(value, u):
        target = value.astype(BF16)
        target_ref[:, u * half : (u + 1) * half] = target
        target = target.astype(F32)
        noise = slopes[u, col].astype(F32)
        lanes = pl.ds(pl.multiple_of(col * share + u * half, half), half)
        st = (1.0 - t) * noise + t * target + t * embed_ref[:, lanes]
        latents[u, col] = (st * gain_ref[:, lanes]).astype(BF16)
        state[:, u * half : (u + 1) * half] = st - (target - noise)
        return jnp.sum(st * st, axis=1, keepdims=True)

    begin0, middle0, finish0 = cols_reduce(target_block, 0, 0)
    begin1, middle1, finish1 = cols_reduce(target_block, 0, 1)
    hb0, hm0, hf0, hg0, hc0 = cols_gather(latents, 0, 0)
    hb1, hm1, hf1, hg1, hc1 = cols_gather(latents, 0, 1)
    begin0()
    middle0()
    begin1()
    middle1()
    gather(0, "4")
    part = make_state(finish0(), 0)
    hb0()
    part = part + make_state(finish1(), 1)
    part, _ = flat(part, part)
    rsend[ITERS, 0:1, :] = part
    rsend[ITERS, 1:2, :] = part
    cols_swap(ITERS)
    hm0()
    hb1()
    gather(2, "2a", "2b")
    gather(0, "end")

    def use_latent(i, first=False):
        def step(j, _):
            value = (jnp.dot(latents[0, i], win[rows_of(i, 0, half), tile(j)], preferred_element_type=F32)
                     + jnp.dot(latents[1, i], win[rows_of(i, 1, half), tile(j)], preferred_element_type=F32))
            hid[:, tile(j)] = value if first else hid[:, tile(j)] + value
            return 0

        lax.fori_loop(0, tiles, step, 0)

    use_latent(col, True)
    gather(1, "3a", "3b", "3c")
    hf0()
    hm1()
    hg0(2)
    hg1(2)
    use_latent(slot(0, other))
    use_latent(slot(-1, core))
    hf1()
    use_latent(slot(1, core))
    gather(1, "4")
    hg0(5)
    hg1(5)
    use_latent(slot(-1, other))
    hg0(6)
    hg1(6)
    use_latent(slot(1, other))
    use_latent(slot(2, core))
    gather(2, "3a", "3b", "3c")
    hg0(7, 8)
    hg1(7, 8)
    use_latent(slot(2, other))
    hc0()
    hc1()
    await_all(rrecv.at[ITERS], rr.at[ITERS])
    await_all(rrecv.at[ITERS], rs.at[ITERS])
    square = part + jnp.sum(rrecv[ITERS][:, 0, :], axis=0, keepdims=True)
    scale = tall(lax.rsqrt(square / width + 1e-6), n)

    def gelu_step(j, _):
        h = hid[:, tile(j)] * scale
        c = math.sqrt(2.0 / math.pi)
        h2 = h * h
        th = jnp.tanh(c * (h + 0.044715 * (h2 * h)))
        act[:, tile(j)] = (0.5 * h * (1.0 + th)).astype(BF16)
        slope_of = 0.5 * (1.0 + th) + 0.5 * h * (1.0 - th * th) * (c * (1.0 + (3 * 0.044715) * h2))
        hid[:, tile(j)] = slope_of * scale
        return 0

    lax.fori_loop(0, tiles, gelu_step, 0)
    gather(1, "end")

    def pair(ref, i, u, at):
        lo = ref[pl.ds(pl.multiple_of(i * share + u * eighth, eighth), eighth), at]
        hi = ref[pl.ds(pl.multiple_of(i * share + half + u * eighth, eighth), eighth), at]
        return jnp.concatenate([lo, hi], axis=0)

    def velocity_block(fb, u):
        return lax.dot_general(act[...], pair(wout, fb, u, slice(None)), NT, preferred_element_type=F32)

    def make_slope(value, u):
        lo = state[:, u * eighth : (u + 1) * eighth]
        hi = state[:, half + u * eighth : half + (u + 1) * eighth]
        slopes[u, col] = ((jnp.concatenate([lo, hi], axis=1) + value) * (1.0 / math.sqrt(tokens))).astype(BF16)

    def use_slope(i, u):
        turned[...] = slopes[u, i].astype(F32).T.astype(BF16)

        def step(j, _):
            value = jnp.dot(turned[...], act[:, tile(j)], preferred_element_type=F32).astype(BF16)
            dbuf[pl.ds(pl.multiple_of(i * share + u * eighth, eighth), eighth), tile(j)] = value[:eighth]
            dbuf[pl.ds(pl.multiple_of(i * share + half + u * eighth, eighth), eighth), tile(j)] = value[eighth:]
            return 0

        lax.fori_loop(0, tiles, step, 0)

    def rx_at(ref, base, unit, path, j, part=None):
        high = unit[1]
        off = high // 2 if part == 1 else 0
        size = high if part is None else high // 2
        return ref.at[pl.ds(base + (path * 16 + j) * high + off, size)]

    scatters = {}

    def scatter(w, step):
        ref = (dbuf, dbuf, win)[w]
        unit = (low, up, wide)[w]
        land = (rx, rx, wout)[w]
        base = (0, width // 2, 0)[w]
        high = unit[1]

        def copy(path, i, src, dst, axis, d):
            scatters[w, path, i] = rcopy(src, dst, gr_s.at[w, path, i], gr_r.at[w, path, i], toward(path, axis, d))

        def got(path, i):
            scatters[w, path, i].wait_recv()

        def add(at, *more):
            value = at[...].astype(F32)
            for r in more:
                value = value + r[...].astype(F32)
            at[...] = value.astype(BF16)

        for path in range(2):
            f, s = here(path)
            if step == 1:
                for j, e in enumerate((2, 1)):
                    copy(path, j, piece(ref, unit, path, f + 2, s + e), rx_at(land, base, unit, path, j), "f", 1)
                for j, e in enumerate((3, 0)):
                    copy(path, 2 + j, piece(ref, unit, path, f + 2, s + e), rx_at(land, base, unit, path, 2 + j), "f", -1)
                for e in (3, 0):
                    copy(path, 4 + e, piece(ref, unit, path, f + 1, s + e), rx_at(land, base, unit, path, 4 + e), "f", 1)
                for e in (2, 1):
                    copy(path, 8 + e, piece(ref, unit, path, f - 1, s + e), rx_at(land, base, unit, path, 8 + e), "f", -1)
            if step == 2:
                for j in range(2):
                    e = (2, 1)[j]
                    got(path, j)
                    at = piece(ref, unit, path, f + 1, s + e)
                    add(at, rx_at(land, base, unit, path, j))
                    copy(path, 4 + e, at, rx_at(land, base, unit, path, 4 + e), "f", 1)
                    e = (3, 0)[j]
                    got(path, 2 + j)
                    at = piece(ref, unit, path, f - 1, s + e)
                    add(at, rx_at(land, base, unit, path, 2 + j))
                    copy(path, 8 + e, at, rx_at(land, base, unit, path, 8 + e), "f", -1)
            if step == 3:
                for e in ORDER:
                    got(path, 4 + e)
                    got(path, 8 + e)
                    add(piece(ref, unit, path, f, s + e), rx_at(land, base, unit, path, 4 + e), rx_at(land, base, unit, path, 8 + e))
                    if e == 2:
                        copy(path, 12, piece(ref, unit, path, f, s + 2, 0), rx_at(land, base, unit, path, 12, 0), "s", 1)
                        copy(path, 13, piece(ref, unit, path, f, s + 2, 1), rx_at(land, base, unit, path, 12, 1), "s", -1)
                    if e == 1:
                        copy(path, 14, piece(ref, unit, path, f, s + 1, 1), rx_at(land, base, unit, path, 13, 1), "s", 1)
                    if e == 3:
                        copy(path, 15, piece(ref, unit, path, f, s - 1, 0), rx_at(land, base, unit, path, 14, 0), "s", -1)
            if step == 4:
                got(path, 12)
                at = piece(ref, unit, path, f, s + 1, 0)
                add(at, rx_at(land, base, unit, path, 12, 0))
                copy(path, 16, at, rx_at(land, base, unit, path, 13, 0), "s", 1)
                got(path, 13)
                at = piece(ref, unit, path, f, s - 1, 1)
                add(at, rx_at(land, base, unit, path, 12, 1))
                copy(path, 17, at, rx_at(land, base, unit, path, 14, 1), "s", -1)
            if step == 5:
                for i in range(14, 18):
                    got(path, i)
                value = (piece(ref, unit, path, f, s)[...].astype(F32) + rx_at(land, base, unit, path, 13)[...].astype(F32)
                         + rx_at(land, base, unit, path, 14)[...].astype(F32))
                if w < 2:
                    final[w, path * high : (path + 1) * high, :] = value
                    if path == 1:
                        gout_ref[:, w * 2 * high : (w + 1) * 2 * high] = final[w].T.astype(BF16)
                else:
                    gin_ref[path * high : (path + 1) * high, :] = value.astype(BF16)
                for i in range(18):
                    scatters[w, path, i].wait_send()

    begin0, middle0, finish0 = cols_reduce(velocity_block, 1, 0)
    begin1, middle1, finish1 = cols_reduce(velocity_block, 1, 1)
    sb0, sm0, sf0, sg0, sc0 = cols_gather(slopes, 1, 0)
    sb1, sm1, sf1, sg1, sc1 = cols_gather(slopes, 1, 1)
    begin0()
    middle0()
    gather(2, "4", "end")
    begin1()
    middle1()
    make_slope(finish0(), 0)
    sb0()
    use_slope(col, 0)
    make_slope(finish1(), 1)
    sm0()
    sb1()
    sg0(2)
    use_slope(slot(0, other), 0)
    use_slope(slot(-1, core), 0)
    use_slope(slot(1, core), 0)
    sf0()
    use_slope(slot(2, core), 0)
    sg0(5)
    use_slope(slot(-1, other), 0)
    sg0(6)
    use_slope(slot(1, other), 0)
    sg0(7, 8)
    use_slope(slot(2, other), 0)
    scatter(0, 1)
    sm1()
    use_slope(col, 1)
    sg1(2)
    use_slope(slot(0, other), 1)
    use_slope(slot(-1, core), 1)
    use_slope(slot(1, core), 1)
    sf1()
    use_slope(slot(2, core), 1)
    sg1(5)
    use_slope(slot(-1, other), 1)
    sg1(6)
    use_slope(slot(1, other), 1)
    sg1(7, 8)
    use_slope(slot(2, other), 1)
    scatter(1, 1)
    sc0()
    sc1()
    scatter(0, 2)

    back[...] = jnp.zeros_like(back)

    def back_step(i, _):
        def step(j, _):
            back[:, tile(j)] += (jnp.dot(slopes[0, i], pair(wout, i, 0, tile(j)), preferred_element_type=F32)
                                 + jnp.dot(slopes[1, i], pair(wout, i, 1, tile(j)), preferred_element_type=F32))
            return 0

        return lax.fori_loop(0, tiles, step, 0)

    lax.fori_loop(0, n_cols, back_step, 0)
    for c in gathers.values():
        c.wait_send()
    for path in range(2):
        for d in (1, -1):
            pl.semaphore_signal(credit, inc=1, device_id=toward(path, "f", d), device_id_type=MESH)
    scatter(1, 2)
    sh[...] = (back[...] * hid[...]).astype(BF16)

    def in_step(i, _):
        for u in range(2):
            turned[...] = latents[u, i].astype(F32).T.astype(BF16)

            def step(j, _):
                win[rows_of(i, u, half), tile(j)] = jnp.dot(
                    turned[...], sh[:, tile(j)], preferred_element_type=F32).astype(BF16)
                return 0

            lax.fori_loop(0, tiles, step, 0)
        return 0

    lax.fori_loop(0, n_cols, in_step, 0)
    pl.semaphore_wait(credit, 4)
    scatter(2, 1)
    scatter(0, 3)
    scatter(1, 3)
    scatter(2, 2)
    scatter(0, 4)
    scatter(1, 4)
    scatter(0, 5)
    scatter(1, 5)
    scatter(2, 3)
    scatter(2, 4)
    scatter(2, 5)


def hand_out(a, b, c, x, y, z, sem):
    copies = [pltpu.make_async_copy(s, d, sem.at[i]) for i, (s, d) in enumerate(((a, x), (b, y), (c, z)))]
    for c in copies:
        c.start()
    for c in copies:
        c.wait()


def per_device(noise, data, times, time_embed, norm_gain, w_in, w_out):
    n, width = noise.shape
    m = data.shape[0]
    wr, ffd = w_in.shape
    share = width // 8
    half = share // 2
    vm = pl.BlockSpec(memory_space=pltpu.VMEM)
    hbm = pl.BlockSpec(memory_space=pl.ANY)
    dma = pltpu.SemaphoreType.DMA
    outs = pl.pallas_call(
        kernel,
        out_shape=(
            jax.ShapeDtypeStruct((n, share), BF16),
            jax.ShapeDtypeStruct((wr, ffd), BF16),
            jax.ShapeDtypeStruct((ffd, wr), BF16),
        ),
        in_specs=[hbm, hbm, vm, vm, vm, hbm, vm],
        out_specs=(vm, vm, vm),
        scratch_shapes=[
            pltpu.VMEM((2, 8, n, half), BF16),
            pltpu.VMEM((width, ffd), BF16),
            pltpu.VMEM((width, ffd), BF16),
            pltpu.VMEM((width, ffd), BF16),
            pltpu.VMEM((width, ffd), BF16),
            pltpu.VMEM((2, 8, n, half), BF16),
            pltpu.VMEM((n, ffd), BF16),
            pltpu.VMEM((n, ffd), F32),
            pltpu.VMEM((n, ffd), F32),
            pltpu.VMEM((n, m), F32),
            pltpu.VMEM((n, m), BF16),
            pltpu.VMEM((n, share), F32),
            pltpu.VMEM((n, ffd), BF16),
            pltpu.VMEM((half, n), BF16),
            pltpu.VMEM((2, 4, n, half), BF16),
            pltpu.VMEM((2, 4, n, half), BF16),
            pltpu.VMEM((2, n, half), BF16),
            pltpu.VMEM((2, n, half), BF16),
            pltpu.VMEM((2, n, half), BF16),
            pltpu.VMEM((2, 2, n // 2, half), BF16),
            pltpu.VMEM((2, 2, n, half), BF16),
            pltpu.VMEM((2, n, half), F32),
            pltpu.VMEM((n, 128), F32),
            pltpu.VMEM((m, 128), F32),
            pltpu.VMEM((2, wr // 2, ffd), F32),
            pltpu.VMEM((ITERS, 2, m), F32),
            pltpu.VMEM((ITERS, 15, 2, m), F32),
            pltpu.VMEM((ITERS + 1, 2, n), F32),
            pltpu.VMEM((ITERS + 1, 7, 2, n), F32),
            dma((ITERS,)), dma((ITERS,)), dma((ITERS + 1,)), dma((ITERS + 1,)),
            dma((3, 2, 20)), dma((3, 2, 20)),
            dma((2, 2, 10)), dma((2, 2, 10)),
            dma((2, 2, 9)), dma((2, 2, 9)),
            dma((3, 2, 18)), dma((3, 2, 18)),
            dma((21,)),
            pltpu.SemaphoreType.REGULAR,
        ],
        compiler_params=pltpu.CompilerParams(
            collective_id=0, has_side_effects=True, vmem_limit_bytes=62 * 2**20
        ),
    )(noise, data, times, time_embed[None, :], norm_gain[None, :], w_in, w_out)
    return pl.pallas_call(
        hand_out,
        out_shape=tuple(jax.ShapeDtypeStruct(o.shape, o.dtype) for o in outs),
        in_specs=[hbm] * 3,
        out_specs=(hbm,) * 3,
        scratch_shapes=[dma((3,))],
    )(*outs)


def solution(mesh):
    in_specs = (
        P("rows", None),
        P("cols", None),
        P("rows"),
        P(),
        P(),
        P("rows", "cols"),
        P("cols", "rows"),
    )
    out_specs = (P("rows", "cols"), P("rows", "cols"), P("cols", "rows"))
    return jax.shard_map(
        per_device, mesh=mesh, in_specs=in_specs, out_specs=out_specs, check_vma=False
    )
```

time: 279 us -> 299 us (1.072)
  Pallas kernels: 271 us -> 298 us
  local copies, waits for them, and re-layouts: 6.75 us -> 0 us
    pallas_call x0 -> x1, Pallas kernels: none -> 44.8 us  [per_device(): pl.pallas_call(hand_out, out_shape=tuple((jax.ShapeDtypeStruct(o.shape, o...]
    pallas_call x1, Pallas kernels: 271 us -> 253 us  [per_device(): pl.pallas_call(kernel, out_shape=(jax.ShapeDtypeStruct((n, share), BF16),...]
    unnamed x3 -> x0, local copies, waits for them, and re-layouts: 5.5 us -> none
where the time goes in v3:
time: 299 us; the launch traced here: 298 us
  Pallas kernels  298 us (100%)
    pallas_call x1, Pallas kernels, per_device(): pl.pallas_call(kernel, out_shape=(jax.ShapeDtypeStruct((n, share), BF16),...  253 us
    pallas_call x1, Pallas kernels, per_device(): pl.pallas_call(hand_out, out_shape=tuple((jax.ShapeDtypeStruct(o.shape, o...  44.8 us

profile of v3, /device:TPU:0, one launch (start us, length us, event | category | flops | bytes accessed | tf_op | source)
XLA Modules:
  0.0 298.5 jit_solution(16678071115069496152)
XLA Ops:
  0.6 252.8 %shard_map.94 = (bf16[384,512]{1,0:T(8,128)(2,1)}, bf16[256,1024]{1,0:T(8,128)(2,1)}, bf16[1024,256]{1,0:T(8,128)(2,1)}) custom-call(bf16[384,4096]{1,0:T(8,128)(2,1)} %noise_hbm.1, bf16[768,4096]{1,0:T(8,128)(2,1)} %data_hbm.1, f32[384]{0:T(512)} %times_ref.1, f32[1,4096]{1,0:T(1,128)} %bitcast.2, f32[1,4096]{1,0:T(1,128)} %bitcast.3, ...), custom_call_target="tpu_custom_call" | custom-call | tf_op jit(solution)/shard_map/pallas_call | solution.py:634
  253.5 44.8 %shard_map.95 = (bf16[384,512]{1,0:T(8,128)(2,1)}, bf16[256,1024]{1,0:T(8,128)(2,1)}, bf16[1024,256]{1,0:T(8,128)(2,1)}) custom-call(bf16[384,512]{1,0:T(8,128)(2,1)} %get-tuple-element.6.a, bf16[256,1024]{1,0:T(8,128)(2,1)} %get-tuple-element.7.b, bf16[1024,256]{1,0:T(8,128)(2,1)} %get-tuple-element.8.c), custom_call_target="tpu_custom_call" | custom-call | tf_op jit(solution)/shard_map/pallas_call | solution.py:685

commit v4 on v3

v4 whole, which is shorter than its diff:
```python
import functools
import math

import jax
import jax.numpy as jnp
from jax import lax
from jax.experimental import pallas as pl
from jax.experimental.pallas import tpu as pltpu
from jax.sharding import PartitionSpec as P

ITERS = 3
EPSILON = 0.01
MESH = pl.DeviceIdType.MESH
F32 = jnp.float32
BF16 = jnp.bfloat16
NT = (((1,), (1,)), ((), ()))
ORDER = (2, 1, 3, 0)


def ring(value):
    return lax.rem(value + 4, 4)


def tall(row, rows):
    return jnp.broadcast_to(row, (128, rows)).T[:, 0:1]


def flat(left, right):
    lane = lax.broadcasted_iota(jnp.int32, (left.shape[0], 128), 1)
    both = jnp.where(lane < 64, left, right).T
    return both[0:1], both[64:65]


def kernel(noise_hbm, data_hbm, times_ref, embed_ref, gain_ref, w_in_hbm, w_out_ref,
           target_ref, gin_ref, gout_ref,
           slopes, dbuf, win, wout, rx, latents, act, hid, back, a_ref, p_ref, state, sh,
           sibs, sibr, outs, rh, rf, own, nsq, dsq, final,
           csend, crecv, rsend, rrecv,
           cs, cr, rs, rr, ag_s, ag_r, xs, xr, ug_s, ug_r, gr_s, gr_r, loc, credit):
    n_rows, n_cols = 16, 8
    row = lax.axis_index("rows")
    col = lax.axis_index("cols")
    z, y = row // 4, lax.rem(row, 4)
    xx, core = col // 2, lax.rem(col, 2)
    n, width = noise_hbm.shape
    m = data_hbm.shape[0]
    share = width // n_cols
    wr, ffd = w_in_hbm.shape
    half = share // 2
    eighth = share // 4
    hn = n // 2
    tokens = n * n_rows

    def rdesc(src, dst, send, recv, to):
        return pltpu.make_async_remote_copy(src_ref=src, dst_ref=dst, send_sem=send, recv_sem=recv,
                                            device_id=to, device_id_type=MESH)

    def rcopy(*args):
        rdesc(*args).start()

    barrier = pltpu.get_barrier_semaphore()
    for d in range(1, n_rows):
        pl.semaphore_signal(barrier, inc=1, device_id=(lax.rem(row + d, n_rows), col), device_id_type=MESH)
    for d in range(1, n_cols):
        pl.semaphore_signal(barrier, inc=1, device_id=(row, lax.rem(col + d, n_cols)), device_id_type=MESH)

    def mine(i):
        return pl.ds(pl.multiple_of(i * wr, wr), wr)

    w_copy = pltpu.make_async_copy(w_in_hbm, win.at[mine(row)], loc.at[0])
    w_copy.start()

    def noise_copy(q):
        return pltpu.make_async_copy(noise_hbm.at[:, pl.ds(pl.multiple_of(q * half, half), half)],
                                     slopes.at[lax.rem(q, 2), q // 2], loc.at[5 + q])

    def data_copy(q):
        return pltpu.make_async_copy(data_hbm.at[:, pl.ds(pl.multiple_of(q * 2 * share, 2 * share), 2 * share)],
                                     dbuf.at[pl.ds(pl.multiple_of(q * m, m), m)], loc.at[1 + q])

    for q in range(4):
        for h in range(4):
            noise_copy(4 * q + h).start()
        data_copy(q).start()
    wout[mine(row)] = w_out_ref[...].astype(F32).T.astype(BF16)
    w_copy.wait()

    def place(path, f, s):
        return s * 4 + f if path == 0 else f * 4 + s

    def here(path):
        return (y, z) if path == 0 else (z, y)

    def piece(ref, unit, path, f, s, part=None):
        base, high = unit
        off = base + path * high + (high // 2 if part == 1 else 0)
        size = high if part is None else high // 2
        return ref.at[pl.ds(pl.multiple_of(place(path, ring(f), ring(s)) * wr + off, high // 2), size)]

    wide, low, up = (0, wr // 2), (0, wr // 4), (wr // 2, wr // 4)

    def toward(path, axis, d):
        f, s = here(path)
        if axis == "f":
            return (place(path, ring(f + d), s), col)
        return (place(path, f, ring(s + d)), col)

    routes = [
        ("f", 1, 0, 0, None), ("f", -1, 0, 0, None), ("s", 1, 0, 0, None), ("s", -1, 0, 0, None),
        ("f", 1, -1, 0, 0), ("f", -1, 1, 0, 1),
        ("s", 1, -1, 0, None), ("s", -1, -1, 0, None), ("s", 1, 1, 0, None), ("s", -1, 1, 0, None),
        ("s", 1, 0, -1, 0), ("s", -1, 0, 1, 1), ("s", 1, 2, 0, None), ("s", -1, 2, 0, None),
        ("s", 1, -1, -1, 0), ("s", -1, -1, 1, 1), ("s", 1, 1, -1, 0), ("s", -1, 1, 1, 1),
        ("s", 1, 2, -1, 0), ("s", -1, 2, 1, 1),
    ]

    def carry(w, path, i):
        axis, d, df, ds_, part = routes[i]
        f, s = here(path)
        spot = piece((win, wout, wout)[w], (wide, low, up)[w], path, f + df, s + ds_, part)
        return rdesc(spot, spot, ag_s.at[w, path, i], ag_r.at[w, path, i], toward(path, axis, d))

    sends = {"1": (0, 1, 2, 3), "2a": (4, 5, 6, 7, 8, 9), "2b": (10, 11), "3a": (12, 13), "3b": (14, 15),
             "3c": (16, 17), "4": (18, 19)}
    needs = {"2a": (0, 1), "2b": (2, 3), "3a": (4, 5), "3b": (6, 7), "3c": (8, 9), "4": (12, 13),
             "end": (10, 11, 14, 15, 16, 17, 18, 19)}

    def gather(w, *steps):
        for step in steps:
            for i in needs.get(step, ()):
                for path in range(2):
                    carry(w, path, i).wait_recv()
            for i in sends.get(step, ()):
                for path in range(2):
                    carry(w, path, i).start()

    plan = {
        "p0": [(0,"1"), (1,"1")],
        "c4": [(0,"2a","2b")],
        "k0r": [(2,"1")],
        "k1c": [(0,"3a")],
        "k1r": [(0,"3b")],
        "k2c": [(0,"3c"), (1,"2a")],
        "k2r": [(1,"2b"), (0,"4")],
        "t0": [(2,"2a")],
        "t2": [(2,"2b"), (1,"3a")],
        "t4": [(1,"3b")],
        "t5": [(1,"3c")],
        "h0": [(0,"end")],
        "h1": [(2,"3a"), (1,"4")],
        "h2": [(2,"3b"), (2,"3c")],
        "h4": [(2,"4")],
        "v0": [(1,"end")],
        "v1": [(2,"end")],
    }

    def at(point):
        for job in plan.get(point, ()):
            gather(*job)

    pl.semaphore_wait(barrier, n_rows + n_cols - 2)
    at("p0")

    def squares(value):
        value = value.astype(F32)
        value = value * value
        out = value[:, 0:128]
        for j in range(1, value.shape[1] // 128):
            out = out + value[:, j * 128 : (j + 1) * 128]
        return out

    a_ref[...] = jnp.zeros_like(a_ref)
    nsq[...] = jnp.zeros_like(nsq)
    dsq[...] = jnp.zeros_like(dsq)

    def cost_step(q, _):
        for h in range(4):
            noise_copy(4 * q + h).wait()
        data_copy(q).wait()
        total = None
        for h in range(4):
            term = lax.dot_general(slopes[h % 2, 2 * q + h // 2],
                                   dbuf[pl.ds(pl.multiple_of(q * m, m), m), h * half : (h + 1) * half], NT,
                                   preferred_element_type=F32)
            total = term if total is None else total + term
        a_ref[...] += total

        def noise_rows(i, _):
            at = pl.ds(pl.multiple_of(i * 32, 32), 32)
            value = squares(slopes[0, 2 * q, at, :])
            for h in range(1, 4):
                value = value + squares(slopes[h % 2, 2 * q + h // 2, at, :])
            nsq[at, :] += value
            return 0

        def data_rows(i, _):
            at = pl.ds(pl.multiple_of(i * 32, 32), 32)
            dsq[at, :] += squares(dbuf[pl.ds(pl.multiple_of(q * m + i * 32, 32), 32), :])
            return 0

        lax.fori_loop(0, n // 32, noise_rows, 0)
        lax.fori_loop(0, m // 32, data_rows, 0)
        return 0

    lax.fori_loop(0, 4, cost_step, 0)
    noise_sq = jnp.sum(nsq[...], axis=1, keepdims=True)
    data_sq = jnp.sum(dsq[...].T, axis=0, keepdims=True)
    a_ref[...] = (noise_sq + data_sq - 2.0 * a_ref[...]) * (1.0 / (width * EPSILON))
    base = -math.log(tokens)
    at("c4")

    def rows_swap(it):
        for d in range(1, n_rows):
            rcopy(csend.at[it], crecv.at[it, d - 1], cs.at[it], cr.at[it], (lax.rem(row + d, n_rows), col))

    def cols_swap(it):
        for d in range(1, n_cols):
            rcopy(rsend.at[it], rrecv.at[it, d - 1], rs.at[it], rr.at[it], (row, lax.rem(col + d, n_cols)))

    def await_all(ref, sem):
        pltpu.make_async_copy(ref, ref, sem).wait()

    def merge(got, top, tot):
        gt = got[:, 0, :]
        best = jnp.maximum(top, jnp.max(gt, axis=0, keepdims=True))
        total = tot * jnp.exp(top - best) + jnp.sum(got[:, 1, :] * jnp.exp(gt - best), axis=0, keepdims=True)
        return base - (best + jnp.log(total))

    def when(condition, *points):
        @pl.when(condition)
        def _():
            for point in points:
                at(point)

    def sweep(it, fg):
        x = fg[0] - a_ref[...]
        top = jnp.max(x, axis=0, keepdims=True)
        tot = jnp.sum(jnp.exp(x - top), axis=0, keepdims=True)
        csend[it, 0:1, :] = top
        csend[it, 1:2, :] = tot
        rows_swap(it)
        for i in range(ITERS):
            when(it == i, ("k0c", "k1c", "k2c")[i])
        await_all(crecv.at[it], cr.at[it])
        g = merge(crecv[it], top, tot)

        x = g - a_ref[...]
        top = jnp.max(x, axis=1, keepdims=True)
        tot = jnp.sum(jnp.exp(x - top), axis=1, keepdims=True)
        top, tot = flat(top, tot)
        rsend[it, 0:1, :] = top
        rsend[it, 1:2, :] = tot
        cols_swap(it)
        for i in range(ITERS):
            when(it == i, ("k0r", "k1r", "k2r")[i])
        await_all(rrecv.at[it], rr.at[it])
        return tall(merge(rrecv[it], top, tot), n), g

    f, g = lax.fori_loop(0, ITERS, sweep, (jnp.zeros((n, 1), F32), jnp.zeros((1, m), F32)))
    p_ref[...] = (float(tokens) * jnp.exp(f + g - a_ref[...])).astype(BF16)
    for it in range(ITERS):
        await_all(crecv.at[it], cs.at[it])
        await_all(rrecv.at[it], rs.at[it])

    def at_x(d, k):
        return (row, ring(xx + d) * 2 + k)

    def reduce_copy(t, u, i):
        lo, hi = pl.ds(0, hn), pl.ds(hn, hn)
        if not isinstance(i, int):
            src, dst, to = sibs.at[u, i], sibr.at[u, i], at_x(0, 1 - core)
        else:
            src, dst, d = {
                4: (outs.at[u, 0, lo], rh.at[u, 0], 1),
                5: (outs.at[u, 0, hi], rh.at[u, 1], -1),
                6: (outs.at[u, 1, hi], rf.at[u, 0, hi], 1),
                7: (outs.at[u, 2, lo], rf.at[u, 1, lo], -1),
                8: (outs.at[u, 1, lo], rf.at[u, 0, lo], 1),
                9: (outs.at[u, 2, hi], rf.at[u, 1, hi], -1),
            }[i]
            to = at_x(d, core)
        return rdesc(src, dst, xs.at[t, u, i], xr.at[t, u, i], to)

    def cols_reduce(make, t, u):
        def block_step(i, _):
            d = jnp.where(i == 0, 2, jnp.where(i == 3, 0, 2 * i - 1))
            sibs[u, i] = make(ring(xx + d) * 2 + 1 - core, u).astype(BF16)
            reduce_copy(t, u, i).start()
            value = make(ring(xx + d) * 2 + core, u)
            reduce_copy(t, u, i).wait_recv()
            value = value + sibr[u, i].astype(F32)
            own[u] = value
            outs[u, i] = value.astype(BF16)

            @pl.when(i == 0)
            def _():
                reduce_copy(t, u, 4).start()
                reduce_copy(t, u, 5).start()

            @pl.when(i == 1)
            def _():
                reduce_copy(t, u, 6).start()

            @pl.when(i == 2)
            def _():
                reduce_copy(t, u, 7).start()

            return 0

        lax.fori_loop(0, 4, block_step, 0)
        reduce_copy(t, u, 4).wait_recv()
        outs[u, 1, 0:hn] = (outs[u, 1, 0:hn].astype(F32) + rh[u, 0].astype(F32)).astype(BF16)
        reduce_copy(t, u, 8).start()
        reduce_copy(t, u, 5).wait_recv()
        outs[u, 2, hn:n] = (outs[u, 2, hn:n].astype(F32) + rh[u, 1].astype(F32)).astype(BF16)
        reduce_copy(t, u, 9).start()

    def reduced(t, u):
        for i in (6, 7, 8, 9):
            reduce_copy(t, u, i).wait_recv()
        value = own[u] + rf[u, 0].astype(F32) + rf[u, 1].astype(F32)
        for i in range(4):
            reduce_copy(t, u, jnp.int32(i)).wait_send()
        for i in range(4, 10):
            reduce_copy(t, u, i).wait_send()
        return value

    def slot(d, k):
        return ring(xx + d) * 2 + k

    other = 1 - core

    def visit(j):
        d = jnp.where(j < 2, 0, jnp.where(j >= 6, 2, 2 * lax.rem(j, 2) - 1))
        k = jnp.where((j == 1) | (j == 4) | (j == 5) | (j == 7), other, core)
        return slot(d, k)

    def spread(ref, t, u):
        def copy(i):
            lo, hi = pl.ds(0, hn), pl.ds(hn, hn)
            twin = at_x(0, other)
            src, to = {
                0: (ref.at[u, col], at_x(1, core)),
                1: (ref.at[u, col], at_x(-1, core)),
                2: (ref.at[u, col], twin),
                3: (ref.at[u, slot(-1, core), lo], at_x(1, core)),
                4: (ref.at[u, slot(1, core), hi], at_x(-1, core)),
                5: (ref.at[u, slot(-1, core)], twin),
                6: (ref.at[u, slot(1, core)], twin),
                7: (ref.at[u, slot(2, core), lo], twin),
                8: (ref.at[u, slot(2, core), hi], twin),
            }[i]
            return rdesc(src, src, ug_s.at[t, u, i], ug_r.at[t, u, i], to)

        def begin():
            for i in range(3):
                copy(i).start()

        def middle():
            copy(0).wait_recv()
            copy(3).start()
            copy(5).start()
            copy(1).wait_recv()
            copy(4).start()
            copy(6).start()

        def finish():
            copy(3).wait_recv()
            copy(7).start()
            copy(4).wait_recv()
            copy(8).start()

        def got(*which):
            for i in which:
                copy(i).wait_recv()

        def close():
            for i in range(9):
                copy(i).wait_send()

        return begin, middle, finish, got, close

    tiles = ffd // 256

    def tile(j):
        return pl.ds(pl.multiple_of(j * 256, 256), 256)

    def rows_of(i, u, size):
        return pl.ds(pl.multiple_of(i * share + u * size, size), size)

    def target_block(fb, u):
        rows_at = pl.ds(pl.multiple_of(fb // 2 * m, m), m)
        lanes = pl.ds(pl.multiple_of(lax.rem(fb, 2) * share + u * half, half), half)
        return jnp.dot(p_ref[...], dbuf[rows_at, lanes], preferred_element_type=F32)

    t = tall(times_ref[...][None, :], n)

    def make_state(value, u):
        target = value.astype(BF16)
        target_ref[:, u * half : (u + 1) * half] = target
        target = target.astype(F32)
        noise = slopes[u, col].astype(F32)
        lanes = pl.ds(pl.multiple_of(col * share + u * half, half), half)
        st = (1.0 - t) * noise + t * target + t * embed_ref[:, lanes]
        latents[u, col] = (st * gain_ref[:, lanes]).astype(BF16)
        state[:, u * half : (u + 1) * half] = st - (target - noise)
        return jnp.sum(st * st, axis=1, keepdims=True)

    hb0, hm0, hf0, hg0, hc0 = spread(latents, 0, 0)
    hb1, hm1, hf1, hg1, hc1 = spread(latents, 0, 1)

    def target_half(u, _):
        when(u == 0, "t0")
        when(u == 1, "t2")
        cols_reduce(target_block, 0, u)
        return 0

    lax.fori_loop(0, 2, target_half, 0)
    at("t4")
    part = make_state(reduced(0, 0), 0)
    hb0()
    at("t5")
    part = part + make_state(reduced(0, 1), 1)
    part, _ = flat(part, part)
    rsend[ITERS, 0:1, :] = part
    rsend[ITERS, 1:2, :] = part
    cols_swap(ITERS)
    hm0()
    hb1()
    at("h0")
    hid[...] = jnp.zeros_like(hid)

    def hidden_step(j, _):
        @pl.when(j == 1)
        def _():
            at("h1")
            hf0()
            hm1()
            at("h2")
            hg0(2)
            hg1(2)

        @pl.when(j == 3)
        def _():
            hf1()

        @pl.when(j == 4)
        def _():
            at("h3")
            hg0(5)
            hg1(5)

        @pl.when(j == 5)
        def _():
            hg0(6)
            hg1(6)

        @pl.when(j == 7)
        def _():
            at("h4")
            hg0(7, 8)
            hg1(7, 8)

        i = visit(j)
        hid[...] += (jnp.dot(latents[0, i], win[rows_of(i, 0, half), :], preferred_element_type=F32)
                     + jnp.dot(latents[1, i], win[rows_of(i, 1, half), :], preferred_element_type=F32))
        return 0

    lax.fori_loop(0, n_cols, hidden_step, 0)
    hc0()
    hc1()
    await_all(rrecv.at[ITERS], rr.at[ITERS])
    await_all(rrecv.at[ITERS], rs.at[ITERS])
    square = part + jnp.sum(rrecv[ITERS][:, 0, :], axis=0, keepdims=True)
    scale = tall(lax.rsqrt(square / width + 1e-6), n)

    def gelu_step(j, _):
        h = hid[:, tile(j)] * scale
        c = math.sqrt(2.0 / math.pi)
        h2 = h * h
        th = jnp.tanh(c * (h + 0.044715 * (h2 * h)))
        act[:, tile(j)] = (0.5 * h * (1.0 + th)).astype(BF16)
        slope_of = 0.5 * (1.0 + th) + 0.5 * h * (1.0 - th * th) * (c * (1.0 + (3 * 0.044715) * h2))
        hid[:, tile(j)] = slope_of * scale
        return 0

    lax.fori_loop(0, tiles, gelu_step, 0)
    at("v0")

    def pair(ref, i, u, at):
        lo = ref[pl.ds(pl.multiple_of(i * share + u * eighth, eighth), eighth), at]
        hi = ref[pl.ds(pl.multiple_of(i * share + half + u * eighth, eighth), eighth), at]
        return jnp.concatenate([lo, hi], axis=0)

    def velocity_block(fb, u):
        return lax.dot_general(act[...], pair(wout, fb, u, slice(None)), NT, preferred_element_type=F32)

    def make_slope(value, u):
        lo = state[:, u * eighth : (u + 1) * eighth]
        hi = state[:, half + u * eighth : half + (u + 1) * eighth]
        slopes[u, col] = ((jnp.concatenate([lo, hi], axis=1) + value) * (1.0 / math.sqrt(tokens))).astype(BF16)

    TN = (((0,), (0,)), ((), ()))

    def use_slope(i, u):
        value = lax.dot_general(slopes[u, i], act[...], TN, preferred_element_type=F32).astype(BF16)
        dbuf[pl.ds(pl.multiple_of(i * share + u * eighth, eighth), eighth), :] = value[:eighth]
        dbuf[pl.ds(pl.multiple_of(i * share + half + u * eighth, eighth), eighth), :] = value[eighth:]

    def rx_at(ref, base, unit, path, j, part=None):
        high = unit[1]
        off = high // 2 if part == 1 else 0
        size = high if part is None else high // 2
        return ref.at[pl.ds(base + (path * 16 + j) * high + off, size)]

    def shift(w, path, i):
        ref = (dbuf, dbuf, win)[w]
        unit = (low, up, wide)[w]
        f, s = here(path)
        if i < 4:
            e, axis, d = (2, 1, 3, 0)[i], "f", 1 if i < 2 else -1
            src, dst = (f + 2, s + e, None), (i, None)
        elif i < 12:
            e, axis, d = i % 4, "f", 1 if i < 8 else -1
            src, dst = (f + d, s + e, None), (i, None)
        else:
            axis, d = "s", 1 if i % 2 == 0 else -1
            src, dst = {
                12: ((f, s + 2, 0), (12, 0)), 13: ((f, s + 2, 1), (12, 1)),
                14: ((f, s + 1, 1), (13, 1)), 15: ((f, s - 1, 0), (14, 0)),
                16: ((f, s + 1, 0), (13, 0)), 17: ((f, s - 1, 1), (14, 1)),
            }[i]
        return rdesc(piece(ref, unit, path, *src), landing(w, path, *dst),
                     gr_s.at[w, path, i], gr_r.at[w, path, i], toward(path, axis, d))

    def landing(w, path, j, part=None):
        return rx_at((rx, rx, wout)[w], (0, width // 2, 0)[w], (low, up, wide)[w], path, j, part)

    def add(at, *more):
        def rows_step(r, _):
            rows = pl.ds(pl.multiple_of(r * 32, 32), 32)
            value = at[rows, :].astype(F32)
            for one in more:
                value = value + one[rows, :].astype(F32)
            at[rows, :] = value.astype(BF16)
            return 0

        lax.fori_loop(0, at.shape[0] // 32, rows_step, 0)

    def scatter(w, step):
        ref = (dbuf, dbuf, win)[w]
        unit = (low, up, wide)[w]
        high = unit[1]
        if step == 1:
            for i in (0, 1, 2, 3, 4, 7, 9, 10):
                for path in range(2):
                    shift(w, path, i).start()
        for path in range(2):
            f, s = here(path)
            if step == 2:
                for j in range(2):
                    for d, i, e in ((1, j, (2, 1)[j]), (-1, 2 + j, (3, 0)[j])):
                        shift(w, path, i).wait_recv()
                        add(piece(ref, unit, path, f + d, s + e), landing(w, path, i))
                        shift(w, path, (4 if d == 1 else 8) + e).start()
            if step == 3:
                for e in ORDER:
                    shift(w, path, 4 + e).wait_recv()
                    shift(w, path, 8 + e).wait_recv()
                    add(piece(ref, unit, path, f, s + e), landing(w, path, 4 + e), landing(w, path, 8 + e))
                    for i in {2: (12, 13), 1: (14,), 3: (15,), 0: ()}[e]:
                        shift(w, path, i).start()
            if step == 4:
                shift(w, path, 12).wait_recv()
                add(piece(ref, unit, path, f, s + 1, 0), landing(w, path, 12, 0))
                shift(w, path, 16).start()
                shift(w, path, 13).wait_recv()
                add(piece(ref, unit, path, f, s - 1, 1), landing(w, path, 12, 1))
                shift(w, path, 17).start()
            if step == 5:
                for i in range(14, 18):
                    shift(w, path, i).wait_recv()
                value = (piece(ref, unit, path, f, s)[...].astype(F32) + landing(w, path, 13)[...].astype(F32)
                         + landing(w, path, 14)[...].astype(F32))
                if w < 2:
                    final[w, path * high : (path + 1) * high, :] = value
                    if path == 1:
                        gout_ref[:, w * 2 * high : (w + 1) * 2 * high] = final[w].T.astype(BF16)
                else:
                    gin_ref[path * high : (path + 1) * high, :] = value.astype(BF16)
                for i in range(18):
                    shift(w, path, i).wait_send()

    sb0, sm0, sf0, sg0, sc0 = spread(slopes, 1, 0)
    sb1, sm1, sf1, sg1, sc1 = spread(slopes, 1, 1)

    def velocity_half(u, _):
        when(u == 1, "v1")
        cols_reduce(velocity_block, 1, u)
        return 0

    lax.fori_loop(0, 2, velocity_half, 0)
    make_slope(reduced(1, 0), 0)
    sb0()

    def slope_step(jj, _):
        def on(number, *calls):
            @pl.when(jj == number)
            def _():
                for call in calls:
                    call()

        on(1, lambda: make_slope(reduced(1, 1), 1), sm0, sb1, lambda: sg0(2))
        on(4, sf0, lambda: sg0(5))
        on(5, lambda: sg0(6))
        on(7, lambda: sg0(7, 8))
        on(8, lambda: scatter(0, 1), sm1)
        on(9, lambda: sg1(2))
        on(12, sf1, lambda: sg1(5))
        on(13, lambda: sg1(6))
        on(15, lambda: sg1(7, 8))
        use_slope(visit(lax.rem(jj, 8)), jj // 8)
        return 0

    lax.fori_loop(0, 16, slope_step, 0)
    scatter(1, 1)
    sc0()
    sc1()
    scatter(0, 2)

    every = slice(None)
    back[...] = jnp.zeros_like(back)

    def back_step(i, _):
        back[...] += (jnp.dot(slopes[0, i], pair(wout, i, 0, every), preferred_element_type=F32)
                      + jnp.dot(slopes[1, i], pair(wout, i, 1, every), preferred_element_type=F32))
        return 0

    lax.fori_loop(0, n_cols, back_step, 0)
    for w in range(3):
        for path in range(2):
            for i in range(20):
                carry(w, path, i).wait_send()
    for path in range(2):
        for d in (1, -1):
            pl.semaphore_signal(credit, inc=1, device_id=toward(path, "f", d), device_id_type=MESH)
    scatter(1, 2)
    sh[...] = (back[...] * hid[...]).astype(BF16)

    def in_step(i, _):
        win[pl.ds(pl.multiple_of(i * half, half), half), :] = lax.dot_general(
            latents[lax.rem(i, 2), i // 2], sh[...], TN, preferred_element_type=F32).astype(BF16)
        return 0

    lax.fori_loop(0, 2 * n_cols, in_step, 0)
    pl.semaphore_wait(credit, 4)
    scatter(2, 1)
    scatter(0, 3)
    scatter(1, 3)
    scatter(2, 2)
    scatter(0, 4)
    scatter(1, 4)
    scatter(0, 5)
    scatter(1, 5)
    scatter(2, 3)
    scatter(2, 4)
    scatter(2, 5)


def hand_out(a, b, c, x, y, z, *rest):
    sem = rest[3]
    ins = [pltpu.make_async_copy(s, v, sem.at[i]) for i, (s, v) in enumerate(zip((a, b, c), rest))]
    outs = [pltpu.make_async_copy(v, d, sem.at[3 + i]) for i, (v, d) in enumerate(zip(rest, (x, y, z)))]
    for c in ins:
        c.start()
    for i in range(3):
        ins[i].wait()
        outs[i].start()
    for c in outs:
        c.wait()


def per_device(noise, data, times, time_embed, norm_gain, w_in, w_out):
    n, width = noise.shape
    m = data.shape[0]
    wr, ffd = w_in.shape
    share = width // 8
    half = share // 2
    vm = pl.BlockSpec(memory_space=pltpu.VMEM)
    hbm = pl.BlockSpec(memory_space=pl.ANY)
    dma = pltpu.SemaphoreType.DMA
    outs = pl.pallas_call(
        kernel,
        out_shape=(
            jax.ShapeDtypeStruct((n, share), BF16),
            jax.ShapeDtypeStruct((wr, ffd), BF16),
            jax.ShapeDtypeStruct((ffd, wr), BF16),
        ),
        in_specs=[hbm, hbm, vm, vm, vm, hbm, vm],
        out_specs=(vm, vm, vm),
        scratch_shapes=[
            pltpu.VMEM((2, 8, n, half), BF16),
            pltpu.VMEM((width, ffd), BF16),
            pltpu.VMEM((width, ffd), BF16),
            pltpu.VMEM((width, ffd), BF16),
            pltpu.VMEM((width, ffd), BF16),
            pltpu.VMEM((2, 8, n, half), BF16),
            pltpu.VMEM((n, ffd), BF16),
            pltpu.VMEM((n, ffd), F32),
            pltpu.VMEM((n, ffd), F32),
            pltpu.VMEM((n, m), F32),
            pltpu.VMEM((n, m), BF16),
            pltpu.VMEM((n, share), F32),
            pltpu.VMEM((n, ffd), BF16),
            pltpu.VMEM((2, 4, n, half), BF16),
            pltpu.VMEM((2, 4, n, half), BF16),
            pltpu.VMEM((2, 4, n, half), BF16),
            pltpu.VMEM((2, 2, n // 2, half), BF16),
            pltpu.VMEM((2, 2, n, half), BF16),
            pltpu.VMEM((2, n, half), F32),
            pltpu.VMEM((n, 128), F32),
            pltpu.VMEM((m, 128), F32),
            pltpu.VMEM((2, wr // 2, ffd), F32),
            pltpu.VMEM((ITERS, 2, m), F32),
            pltpu.VMEM((ITERS, 15, 2, m), F32),
            pltpu.VMEM((ITERS + 1, 2, n), F32),
            pltpu.VMEM((ITERS + 1, 7, 2, n), F32),
            dma((ITERS,)), dma((ITERS,)), dma((ITERS + 1,)), dma((ITERS + 1,)),
            dma((3, 2, 20)), dma((3, 2, 20)),
            dma((2, 2, 10)), dma((2, 2, 10)),
            dma((2, 2, 9)), dma((2, 2, 9)),
            dma((3, 2, 18)), dma((3, 2, 18)),
            dma((21,)),
            pltpu.SemaphoreType.REGULAR,
        ],
        compiler_params=pltpu.CompilerParams(
            collective_id=0, has_side_effects=True, vmem_limit_bytes=62 * 2**20
        ),
    )(noise, data, times, time_embed[None, :], norm_gain[None, :], w_in, w_out)
    return pl.pallas_call(
        hand_out,
        out_shape=tuple(jax.ShapeDtypeStruct(o.shape, o.dtype) for o in outs),
        in_specs=[hbm] * 3,
        out_specs=(hbm,) * 3,
        scratch_shapes=[pltpu.VMEM(o.shape, o.dtype) for o in outs] + [dma((6,))],
    )(*outs)


def solution(mesh):
    in_specs = (
        P("rows", None),
        P("cols", None),
        P("rows"),
        P(),
        P(),
        P("rows", "cols"),
        P("cols", "rows"),
    )
    out_specs = (P("rows", "cols"), P("rows", "cols"), P("cols", "rows"))
    return jax.shard_map(
        per_device, mesh=mesh, in_specs=in_specs, out_specs=out_specs, check_vma=False
    )
```

time: 299 us -> 246 us (0.82)
  Pallas kernels: 298 us -> 245 us
    pallas_call x1, Pallas kernels: 44.8 us -> 2.18 us  [per_device(): pl.pallas_call(hand_out, out_shape=tuple((jax.ShapeDtypeStruct(o.shape, o...]
    pallas_call x1, Pallas kernels: 253 us -> 243 us  [per_device(): pl.pallas_call(kernel, out_shape=(jax.ShapeDtypeStruct((n, share), BF16),...]
where the time goes in v4:
time: 246 us
  Pallas kernels  245 us (100%)
    pallas_call x1, Pallas kernels, per_device(): pl.pallas_call(kernel, out_shape=(jax.ShapeDtypeStruct((n, share), BF16),...  243 us

profile of v4, /device:TPU:0, one launch (start us, length us, event | category | flops | bytes accessed | tf_op | source)
XLA Modules:
  0.0 245.9 jit_solution(3959362969395870136)
XLA Ops:
  0.6 243.0 %shard_map.94 = (bf16[384,512]{1,0:T(8,128)(2,1)}, bf16[256,1024]{1,0:T(8,128)(2,1)}, bf16[1024,256]{1,0:T(8,128)(2,1)}) custom-call(bf16[384,4096]{1,0:T(8,128)(2,1)} %noise_hbm.1, bf16[768,4096]{1,0:T(8,128)(2,1)} %data_hbm.1, f32[384]{0:T(512)} %times_ref.1, f32[1,4096]{1,0:T(1,128)} %bitcast.2, f32[1,4096]{1,0:T(1,128)} %bitcast.3, ...), custom_call_target="tpu_custom_call" | custom-call | tf_op jit(solution)/shard_map/pallas_call | solution.py:692
  243.7 2.2 shard_map.95

commit v5 on v4

--- a/solution.py
+++ b/solution.py
@@ -121,8 +121,8 @@
         return rdesc(spot, spot, ag_s.at[w, path, i], ag_r.at[w, path, i], toward(path, axis, d))
 
     sends = {"1": (0, 1, 2, 3), "2a": (4, 5, 6, 7, 8, 9), "2b": (10, 11), "3a": (12, 13), "3b": (14, 15),
-             "3c": (16, 17), "4": (18, 19)}
-    needs = {"2a": (0, 1), "2b": (2, 3), "3a": (4, 5), "3b": (6, 7), "3c": (8, 9), "4": (12, 13),
+             "3c": (16, 17), "4": (18, 19), "2x": (4, 5, 6, 7), "2y": (8, 9, 10, 11), "3x": (12, 13, 14, 15)}
+    needs = {"2x": (0, 1), "2y": (2, 3), "3x": (4, 5, 6, 7), "2a": (0, 1), "2b": (2, 3), "3a": (4, 5), "3b": (6, 7), "3c": (8, 9), "4": (12, 13),
              "end": (10, 11, 14, 15, 16, 17, 18, 19)}
 
     def gather(w, *steps):
@@ -136,21 +136,17 @@
 
     plan = {
         "p0": [(0,"1"), (1,"1")],
-        "c4": [(0,"2a","2b")],
-        "k0r": [(2,"1")],
-        "k1c": [(0,"3a")],
-        "k1r": [(0,"3b")],
-        "k2c": [(0,"3c"), (1,"2a")],
-        "k2r": [(1,"2b"), (0,"4")],
-        "t0": [(2,"2a")],
-        "t2": [(2,"2b"), (1,"3a")],
-        "t4": [(1,"3b")],
-        "t5": [(1,"3c")],
-        "h0": [(0,"end")],
-        "h1": [(2,"3a"), (1,"4")],
-        "h2": [(2,"3b"), (2,"3c")],
-        "h4": [(2,"4")],
-        "v0": [(1,"end")],
+        "k0c": [(0,"2x")],
+        "k1c": [(0,"2y")],
+        "k2c": [(0,"3x")],
+        "t0": [(0,"3c"), (2,"1")],
+        "t2": [(0,"4"), (1,"2a","2b")],
+        "t4": [(2,"2x")],
+        "h0": [(0,"end"), (1,"3a","3b","3c"), (2,"2y")],
+        "h2": [(1,"4")],
+        "h3": [(2,"3x")],
+        "h4": [(2,"3c")],
+        "v0": [(2,"4"), (1,"end")],
         "v1": [(2,"end")],
     }
 
@@ -656,14 +652,14 @@
     pl.semaphore_wait(credit, 4)
     scatter(2, 1)
     scatter(0, 3)
+    scatter(2, 2)
     scatter(1, 3)
-    scatter(2, 2)
     scatter(0, 4)
+    scatter(2, 3)
     scatter(1, 4)
+    scatter(2, 4)
     scatter(0, 5)
     scatter(1, 5)
-    scatter(2, 3)
-    scatter(2, 4)
     scatter(2, 5)
 
 

time: 246 us -> 229 us (0.931)
  Pallas kernels: 245 us -> 228 us
    pallas_call x1, Pallas kernels: 243 us -> 225 us  [per_device(): pl.pallas_call(kernel, out_shape=(jax.ShapeDtypeStruct((n, share), BF16),...]
where the time goes in v5:
time: 229 us; the launch traced here: 228 us
  Pallas kernels  228 us (100%)
    pallas_call x1, Pallas kernels, per_device(): pl.pallas_call(kernel, out_shape=(jax.ShapeDtypeStruct((n, share), BF16),...  225 us

profile of v5, /device:TPU:0, one launch (start us, length us, event | category | flops | bytes accessed | tf_op | source)
XLA Modules:
  0.0 228.2 jit_solution(9275952568659482388)
XLA Ops:
  0.6 225.3 %shard_map.94 = (bf16[384,512]{1,0:T(8,128)(2,1)}, bf16[256,1024]{1,0:T(8,128)(2,1)}, bf16[1024,256]{1,0:T(8,128)(2,1)}) custom-call(bf16[384,4096]{1,0:T(8,128)(2,1)} %noise_hbm.1, bf16[768,4096]{1,0:T(8,128)(2,1)} %data_hbm.1, f32[384]{0:T(512)} %times_ref.1, f32[1,4096]{1,0:T(1,128)} %bitcast.2, f32[1,4096]{1,0:T(1,128)} %bitcast.3, ...), custom_call_target="tpu_custom_call" | custom-call | tf_op jit(solution)/shard_map/pallas_call | solution.py:688
  226.0 2.2 shard_map.95

commit v6 on v5

--- a/solution.py
+++ b/solution.py
@@ -278,10 +278,16 @@
         return rdesc(src, dst, xs.at[t, u, i], xr.at[t, u, i], to)
 
     def cols_reduce(make, t, u):
+        def offset(i):
+            return jnp.where(i == 0, 2, jnp.where(i == 3, 0, 2 * i - 1))
+
+        def twin_step(i, _):
+            sibs[u, i] = make(ring(xx + offset(i)) * 2 + 1 - core, u).astype(BF16)
+            reduce_copy(t, u, i).start()
+            return 0
+
         def block_step(i, _):
-            d = jnp.where(i == 0, 2, jnp.where(i == 3, 0, 2 * i - 1))
-            sibs[u, i] = make(ring(xx + d) * 2 + 1 - core, u).astype(BF16)
-            reduce_copy(t, u, i).start()
+            d = offset(i)
             value = make(ring(xx + d) * 2 + core, u)
             reduce_copy(t, u, i).wait_recv()
             value = value + sibr[u, i].astype(F32)
@@ -303,6 +309,7 @@
 
             return 0
 
+        lax.fori_loop(0, 4, twin_step, 0)
         lax.fori_loop(0, 4, block_step, 0)
         reduce_copy(t, u, 4).wait_recv()
         outs[u, 1, 0:hn] = (outs[u, 1, 0:hn].astype(F32) + rh[u, 0].astype(F32)).astype(BF16)

time: 229 us -> 222 us (0.969)
  Pallas kernels: 228 us -> 220 us
    pallas_call x1, Pallas kernels: 225 us -> 218 us  [per_device(): pl.pallas_call(kernel, out_shape=(jax.ShapeDtypeStruct((n, share), BF16),...]
where the time goes in v6:
time: 222 us; the launch traced here: 221 us
  Pallas kernels  220 us (99%)
    pallas_call x1, Pallas kernels, per_device(): pl.pallas_call(kernel, out_shape=(jax.ShapeDtypeStruct((n, share), BF16),...  218 us

profile of v6, /device:TPU:0, one launch (start us, length us, event | category | flops | bytes accessed | tf_op | source)
XLA Modules:
  0.0 220.9 jit_solution(232839286099388182)
XLA Ops:
  0.6 218.1 %shard_map.94 = (bf16[384,512]{1,0:T(8,128)(2,1)}, bf16[256,1024]{1,0:T(8,128)(2,1)}, bf16[1024,256]{1,0:T(8,128)(2,1)}) custom-call(bf16[384,4096]{1,0:T(8,128)(2,1)} %noise_hbm.1, bf16[768,4096]{1,0:T(8,128)(2,1)} %data_hbm.1, f32[384]{0:T(512)} %times_ref.1, f32[1,4096]{1,0:T(1,128)} %bitcast.2, f32[1,4096]{1,0:T(1,128)} %bitcast.3, ...), custom_call_target="tpu_custom_call" | custom-call | tf_op jit(solution)/shard_map/pallas_call | solution.py:695
  218.7 2.2 shard_map.95

commit v7 on v6

--- a/solution.py
+++ b/solution.py
@@ -309,8 +309,15 @@
 
             return 0
 
-        lax.fori_loop(0, 4, twin_step, 0)
-        lax.fori_loop(0, 4, block_step, 0)
+        def twins():
+            lax.fori_loop(0, 4, twin_step, 0)
+
+        def blocks():
+            lax.fori_loop(0, 4, block_step, 0)
+
+        return twins, blocks
+
+    def reduce_middle(t, u):
         reduce_copy(t, u, 4).wait_recv()
         outs[u, 1, 0:hn] = (outs[u, 1, 0:hn].astype(F32) + rh[u, 0].astype(F32)).astype(BF16)
         reduce_copy(t, u, 8).start()
@@ -412,13 +419,16 @@
     hb0, hm0, hf0, hg0, hc0 = spread(latents, 0, 0)
     hb1, hm1, hf1, hg1, hc1 = spread(latents, 0, 1)
 
-    def target_half(u, _):
-        when(u == 0, "t0")
-        when(u == 1, "t2")
-        cols_reduce(target_block, 0, u)
-        return 0
-
-    lax.fori_loop(0, 2, target_half, 0)
+    at("t0")
+    twins0, blocks0 = cols_reduce(target_block, 0, 0)
+    twins1, blocks1 = cols_reduce(target_block, 0, 1)
+    twins0()
+    blocks0()
+    twins1()
+    reduce_middle(0, 0)
+    at("t2")
+    blocks1()
+    reduce_middle(0, 1)
     at("t4")
     part = make_state(reduced(0, 0), 0)
     hb0()
@@ -558,21 +568,23 @@
             for i in (0, 1, 2, 3, 4, 7, 9, 10):
                 for path in range(2):
                     shift(w, path, i).start()
-        for path in range(2):
-            f, s = here(path)
-            if step == 2:
-                for j in range(2):
+        both = [(path, *here(path)) for path in range(2)]
+        if step == 2:
+            for j in range(2):
+                for path, f, s in both:
                     for d, i, e in ((1, j, (2, 1)[j]), (-1, 2 + j, (3, 0)[j])):
                         shift(w, path, i).wait_recv()
                         add(piece(ref, unit, path, f + d, s + e), landing(w, path, i))
                         shift(w, path, (4 if d == 1 else 8) + e).start()
-            if step == 3:
-                for e in ORDER:
+        if step == 3:
+            for e in ORDER:
+                for path, f, s in both:
                     shift(w, path, 4 + e).wait_recv()
                     shift(w, path, 8 + e).wait_recv()
                     add(piece(ref, unit, path, f, s + e), landing(w, path, 4 + e), landing(w, path, 8 + e))
                     for i in {2: (12, 13), 1: (14,), 3: (15,), 0: ()}[e]:
                         shift(w, path, i).start()
+        for path, f, s in both:
             if step == 4:
                 shift(w, path, 12).wait_recv()
                 add(piece(ref, unit, path, f, s + 1, 0), landing(w, path, 12, 0))
@@ -599,7 +611,10 @@
 
     def velocity_half(u, _):
         when(u == 1, "v1")
-        cols_reduce(velocity_block, 1, u)
+        twins, blocks = cols_reduce(velocity_block, 1, u)
+        twins()
+        blocks()
+        reduce_middle(1, u)
         return 0
 
     lax.fori_loop(0, 2, velocity_half, 0)

time: 222 us -> 222 us (level)
  no operation moved by 1% of the time
where the time goes in v7:
time: 222 us; the launch traced here: 221 us
  Pallas kernels  220 us (99%)
    pallas_call x1, Pallas kernels, per_device(): pl.pallas_call(kernel, out_shape=(jax.ShapeDtypeStruct((n, share), BF16),...  218 us

profile of v7, /device:TPU:0, one launch (start us, length us, event | category | flops | bytes accessed | tf_op | source)
XLA Modules:
  0.0 220.7 jit_solution(8612169445716591466)
XLA Ops:
  0.6 217.9 %shard_map.94 = (bf16[384,512]{1,0:T(8,128)(2,1)}, bf16[256,1024]{1,0:T(8,128)(2,1)}, bf16[1024,256]{1,0:T(8,128)(2,1)}) custom-call(bf16[384,4096]{1,0:T(8,128)(2,1)} %noise_hbm.1, bf16[768,4096]{1,0:T(8,128)(2,1)} %data_hbm.1, f32[384]{0:T(512)} %times_ref.1, f32[1,4096]{1,0:T(1,128)} %bitcast.2, f32[1,4096]{1,0:T(1,128)} %bitcast.3, ...), custom_call_target="tpu_custom_call" | custom-call | tf_op jit(solution)/shard_map/pallas_call | solution.py:710
  218.6 2.2 shard_map.95
